TPU v7x, 128 devices: a whole 4x4x4 slice. The times are simulated.
128 devices in a mesh: chk: 8 (over x_lo, z), var: 16 (over x_hi, y, core).
Axes of the slice: x: 4 (x_hi: 2, x_lo: 2; x = x_hi * 2 + x_lo), y: 4, z: 4, core: 2. Of those that a mesh axis runs over, the one named last changes fastest.
Arguments:
- tile_bits: int32 [8, 16, 2, 4096], P('chk', 'var'), may hold values 0 or 1
- tile_pos: int32 [8, 16, 2, 2], P('chk', 'var'), may hold values from 0 to 3, as said below
- tile_count: int32 [8, 16], P('chk', 'var'), may hold values from 1 to 2, as said below
- edge_weight: float32 [8, 16, 2, 4096], P('chk', 'var'), may hold values from 0.1 to 1.9
- syndrome: int32 [2048, 128], P('chk'), may hold values 0 or 1
- channel_prior: float32 [4096], P('var'), may hold values from 1 to 6
- out_cot: float32 [4096, 128], P('var'), may hold values from -0.6 to 0.6
Outputs:
- marginals: float32 [4096, 128], P('var')
- weight_grad: float32 [8, 16, 2, 4096], P('chk', 'var')
- prior_grad: float32 [4096], P('var')
Inputs may be any that keep to these rules, and one draw needn't show every extreme that they name: `tile_pos`: in each grid cell the 2 slots name distinct tiles of its 4 x 4 block grid, check block first. `tile_count`: some grid cell uses all 2 slots.
All inputs are finite; a program needn't handle non-finite values. No bound on the sum of `tile_bits` or of `syndrome` on one device may be relied on, other than what follows from the above.
Results may differ from a plain program's by a relative error of at most 0.0003.
Values sent between devices are 32-bit elements; how exact they have to be, the bound alone decides.
A program may use at most 256 MiB of HBM per device.

v0:
```python
import jax
import jax.numpy as jnp
from jax import lax
from jax.sharding import PartitionSpec as P

TILE = 64
ITERS = 2


DAMP = 0.97
EXACT = lax.Precision.HIGHEST


def linear_both(values, axis):
    length = values.shape[axis]
    pieces = [lax.slice_in_dim(values, index, index + 1, axis=axis) for index in range(length)]
    ones = jnp.ones_like(pieces[0])
    prefix = [ones]
    for index in range(length - 1):
        prefix.append(prefix[-1] * pieces[index])
    suffix = [ones]
    for index in range(length - 1, 0, -1):
        suffix.append(suffix[-1] * pieces[index])
    suffix = suffix[::-1]
    whole = prefix[-1] * pieces[-1]
    return (jnp.concatenate(prefix, axis=axis), jnp.concatenate(suffix, axis=axis), whole)


def exclusive_both(values, axis):
    length = values.shape[axis]
    if length < 16 or length % 8 != 0:
        return linear_both(values, axis)
    shape = values.shape
    split = values.reshape(shape[:axis] + (length // 8, 8) + shape[axis + 1 :])
    inner_before, inner_after, group_whole = linear_both(split, axis + 1)
    outer_before, outer_after, whole = exclusive_both(group_whole, axis)
    before = (inner_before * outer_before).reshape(shape)
    after = (inner_after * outer_after).reshape(shape)
    whole = whole.reshape(shape[:axis] + (1,) + shape[axis + 1 :])
    return (before, after, whole)


def device_tables(bits, positions, count, check_blocks, column_blocks):
    slot_total = bits.shape[0]
    slots = jnp.arange(slot_total, dtype=jnp.int32)
    live = slots < count
    edge = jnp.where(live[:, None], bits, 0).astype(jnp.float32).reshape(slot_total, TILE, TILE)
    row_hot = (positions[:, 0:1] == jnp.arange(check_blocks, dtype=jnp.int32)[None, :]).astype(
        jnp.float32
    )
    col_hot = (positions[:, 1:2] == jnp.arange(column_blocks, dtype=jnp.int32)[None, :]).astype(
        jnp.float32
    )
    same_row = (positions[:, None, 0] == positions[None, :, 0]) & (slots[:, None] != slots[None, :])
    return (edge, row_hot, col_hot, same_row)


def row_products(messages, edge, row_hot, same_row):
    halves = jnp.where(edge[..., None] > 0, jnp.tanh(0.5 * messages), 1.0)
    before, after, whole = exclusive_both(halves, 2)
    whole = whole[:, :, 0, :]
    rows = jnp.prod(jnp.where(row_hot[:, :, None, None] > 0, whole[:, None], 1.0), axis=0)
    others_here = jnp.prod(jnp.where(same_row[:, :, None, None], whole[None], 1.0), axis=1)
    inner = before * after * others_here[:, :, None, :]
    return (inner, rows)


def edge_messages(inner, others, weight, sign_slot, edge, row_hot, col_hot):
    others_slot = jnp.einsum("kc,crs->krs", row_hot, others, precision=EXACT)
    product = sign_slot[:, :, None, :] * inner * others_slot[:, :, None, :]
    update = (edge * weight)[..., None] * jnp.log((1.0 + DAMP * product) / (1.0 - DAMP * product))
    column = jnp.einsum("kv,kcs->vcs", col_hot, jnp.sum(update, axis=1), precision=EXACT)
    return (update, column)


def column_sum(values, col_hot):
    return jnp.einsum("kv,kcs->vcs", col_hot, jnp.sum(values, axis=1), precision=EXACT)


def checks_total(values):
    return lax.psum(values, "chk")


def others_forward(rows, check_blocks):
    own = lax.axis_index("var")
    carry = jnp.ones_like(rows)
    piece = jax.tree.map(lambda part: lax.all_gather(part, "var", axis=0, tiled=True), rows)
    indices = jnp.arange(piece.shape[0], dtype=jnp.int32)
    keep = indices // check_blocks != own
    parts = []
    for block in range(check_blocks):
        pick = (keep & (indices % check_blocks == block))[:, None, None]
        parts.append(carry[block] * jnp.prod(jnp.where(pick, piece, 1.0), axis=0))
    others = jnp.stack(parts)
    return (others, (rows, rows))


def others_backward(rows, grads, check_blocks):
    own = lax.axis_index("var")
    kept_products = jnp.ones_like(rows)
    kept_sums = jnp.zeros_like(rows)
    row_piece = lax.all_gather(rows, "var", axis=0, tiled=True)
    grad_piece = lax.all_gather(grads, "var", axis=0, tiled=True)
    indices = jnp.arange(row_piece.shape[0], dtype=jnp.int32)
    keep = indices // check_blocks != own
    new_products = []
    new_sums = []
    for block in range(check_blocks):
        pick = (keep & (indices % check_blocks == block))[:, None, None]
        factors = jnp.where(pick, row_piece, 1.0)
        weights = jnp.where(pick, grad_piece, 0.0)
        before, after, whole = exclusive_both(factors, 0)
        within = jnp.sum(weights * before * after, axis=0)
        whole = whole[0]
        new_sums.append(kept_sums[block] * whole + kept_products[block] * within)
        new_products.append(kept_products[block] * whole)
    return jnp.stack(new_sums)


def body(tile_bits, tile_pos, tile_count, edge_weight, syndrome, channel_prior, out_cot):
    slot_total = tile_bits.shape[2]
    shots = syndrome.shape[1]
    check_blocks = syndrome.shape[0] // TILE
    column_blocks = channel_prior.shape[0] // TILE
    edge, row_hot, col_hot, same_row = device_tables(
        tile_bits[0, 0], tile_pos[0, 0], tile_count[0, 0], check_blocks, column_blocks
    )
    weight = edge_weight[0, 0].reshape(slot_total, TILE, TILE)
    sign_dev = (1.0 - 2.0 * syndrome.astype(jnp.float32)).reshape(check_blocks, TILE, shots)
    sign_slot = jnp.einsum("kc,crs->krs", row_hot, sign_dev, precision=EXACT)
    prior_dev = channel_prior.reshape(column_blocks, TILE)
    prior_slot = jnp.einsum("kv,vc->kc", col_hot, prior_dev, precision=EXACT)
    messages = jnp.broadcast_to(prior_slot[:, None, :, None], (slot_total, TILE, TILE, shots))
    saved = []
    total = None
    for step in range(ITERS):
        inner, rows = row_products(messages, edge, row_hot, same_row)
        others, kept = others_forward(rows, check_blocks)
        update, column = edge_messages(inner, others, weight, sign_slot, edge, row_hot, col_hot)
        total = prior_dev[:, :, None] + lax.psum(column, "chk")
        saved.append((messages, inner, rows, others, kept))
        if step + 1 < ITERS:
            spread = jnp.einsum("kv,vcs->kcs", col_hot, total, precision=EXACT)
            messages = spread[:, None] - update
    marginals = total.reshape(column_blocks * TILE, shots)
    grad_total = out_cot.reshape(column_blocks, TILE, shots)
    grad_update = jnp.zeros((slot_total, TILE, TILE, shots), jnp.float32)
    prior_grad = jnp.zeros((column_blocks, TILE), jnp.float32)
    weight_grad = jnp.zeros_like(weight)
    for step in reversed(range(ITERS)):
        messages_now, inner, rows, others, kept = saved[step]
        prior_grad = prior_grad + jnp.sum(grad_total, axis=2)

        def message_part(inner_now, others_now, weight_now):
            return edge_messages(
                inner_now, others_now, weight_now, sign_slot, edge, row_hot, col_hot
            )

        unused, pull = jax.vjp(message_part, inner, others, weight)
        grad_inner, grad_others, weight_part = pull((grad_update, grad_total))
        weight_grad = weight_grad + weight_part
        grad_rows = others_backward(rows, grad_others, check_blocks)

        def product_part(messages_in):
            return row_products(messages_in, edge, row_hot, same_row)

        unused_rows, pull_rows = jax.vjp(product_part, messages_now)
        grad_messages = pull_rows((grad_inner, grad_rows))[0]
        grad_total = checks_total(column_sum(grad_messages, col_hot))
        grad_update = -grad_messages
    prior_grad = prior_grad + jnp.sum(grad_total, axis=2)
    return (
        marginals,
        weight_grad.reshape(1, 1, slot_total, TILE * TILE),
        prior_grad.reshape(column_blocks * TILE),
    )


def solution(mesh):
    placed = (
        P("chk", "var", None, None),
        P("chk", "var", None, None),
        P("chk", "var"),
        P("chk", "var", None, None),
        P("chk", None),
        P("var"),
        P("var", None),
    )
    return jax.shard_map(
        body,
        mesh=mesh,
        in_specs=placed,
        out_specs=(P("var", None), P("chk", "var", None, None), P("var")),
        check_vma=False,
    )
```

profile of v0, /device:TPU:0, one launch (start us, length us, event | category | flops | bytes accessed | tf_op | source)
XLA Modules:
  0.0 575.4 jit_solution(4083898244809962754)
XLA Ops:
  14.6 3.7 copy-done.6
  21.0 2.1 copy-done.7
  23.1 2.0 copy-done.19
  45.0 2.1 constant_dynamic-update-slice_fusion.18
  47.1 2.0 constant_dynamic-update-slice_fusion.17
  51.7 25.3 %all-gather.5.cloned.1.call-done = f32[64,64,128]{2,1,0:T(8,128)} async-done(((f32[4,64,128]{2,1,0:T(8,128)}), f32[64,64,128]{2,1,0:T(8,128)}) %all-gather.5.cloned.1.call-update) | async-done | bytes 2097168 | tf_op jit(solution)/shard_map/all_gather | solution.py:87
  77.0 5.0 fusion.84
  83.4 4.1 multiply_reduce_fusion.10
  89.0 1.8 constant_dynamic-update-slice_fusion.198
  90.9 1.8 constant_dynamic-update-slice_fusion.197
  92.7 1.9 constant_dynamic-update-slice_fusion.196
  105.6 2.1 copy-done.13
  125.8 35.2 %all-reduce.45.cloned.1.call-done = f32[4,64,128]{2,0,1:T(4,128)} async-done(((f32[4,64,128]{2,0,1:T(4,128)}), f32[4,64,128]{2,0,1:T(4,128)}) %all-reduce.45.cloned.1.call-update) | async-done | bytes 131088 | tf_op jit(solution)/shard_map/psum | solution.py:140
  162.9 6.1 %fusion.2 = f32[2,64,8,8,128]{4,1,0,3,2:T(8,128)S(1)} fusion(f32[2,8,8,128]{3,0,2,1:T(2,128)S(1)} %bitcast.365, f32[2,64,8,8]{1,0,3,2:T(2,128)S(1)} %copy.293, pred[2,64,8,8]{1,0,3,2:T(4,128)(4,1)S(1)} %copy-done.118, f32[2,64,128]{2,1,0:T(8,128)S(1)} %copy-done.86, f32[2,64,8,8,128]{4,1,0,3,2:T(8,128)} %get-tuple-element.208, ...), kind=kLoop, calls=%fused_computation.34 | loop fusion | flops 11534336 | bytes 8691712 | tf_op jit(solution)/shard_map/jit(_where)/select_n | solution.py:59
  171.4 1.8 constant_dynamic-update-slice_fusion.49
  173.2 2.1 copy-done.23
  178.9 1.7 constant_dynamic-update-slice_fusion.244
  192.8 2.0 constant_dynamic-update-slice_fusion.36
  195.7 1.9 constant_dynamic-update-slice_fusion.34
  200.6 1.9 constant_dynamic-update-slice_fusion.32
  202.5 22.6 %all-gather.7.cloned.1.call-done = f32[64,64,128]{2,1,0:T(8,128)} async-done(((f32[4,64,128]{2,1,0:T(8,128)}), f32[64,64,128]{2,1,0:T(8,128)}) %all-gather.7.cloned.1.call-update) | async-done | bytes 2097168 | tf_op jit(solution)/shard_map/all_gather | solution.py:87
  225.2 5.0 fusion.80
  231.5 6.2 %broadcast_multiply_fusion = (f32[2,64,8,8,128]{4,1,0,3,2:T(8,128)}, f32[2,64,8,8,128]{4,1,0,3,2:T(8,128)S(1)}, f32[2,64,8,8,128]{4,1,0,3,2:T(8,128)S(1)}) fusion(f32[2,64,8,128]{3,1,0,2:T(8,128)} %bitcast.15, f32[2,64,128]{2,1,0:T(8,128)S(1)} %copy-done.124, f32[2,64,128]{2,1,0:T(8,128)S(1)} %copy.302, f32[2,64,128]{2,1,0:T(8,128)S(1)} %copy.295, ...), kind=kLoop, calls=%fused_computation.59 | loop fusion | flops 25165824 | bytes 22446080 | tf_op jit(solution)/shard_map/transpose(jvp())/mul | solution.py:38
  237.7 8.4 %fusion.1 = (f32[2,64,128]{2,1,0:T(8,128)S(1)}, f32[2,64,128]{2,1,0:T(8,128)S(1)}, f32[2,64,8,128]{3,1,0,2:T(8,128)}, f32[2,64,8,128]{3,1,0,2:T(8,128)}, f32[2,6...) fusion(f32[2,64,8,8,128]{4,1,0,3,2:T(8,128)S(1)} %get-tuple-element.118, ...), kind=kLoop, calls=%fused_computation.5 | loop fusion | flops 24870912 | bytes 27721728 | tf_op jit(solution)/shard_map/transpose(jvp())/reduce_sum | solution.py:70
  251.6 1.8 constant_dynamic-update-slice_fusion.166
  253.5 1.8 constant_dynamic-update-slice_fusion.165
  255.3 1.9 constant_dynamic-update-slice_fusion.164
  268.9 1.6 broadcast_multiply_fusion.18
  272.8 1.7 broadcast_multiply_fusion.12
  276.7 1.7 broadcast_multiply_fusion.14
  278.3 1.7 broadcast_multiply_fusion.15
  280.0 1.6 broadcast_multiply_fusion.16
  283.3 14.5 %all-gather.9.cloned.1.call-done = f32[64,64,128]{2,1,0:T(8,128)} async-done(((f32[4,64,128]{2,1,0:T(8,128)}), f32[64,64,128]{2,1,0:T(8,128)}) %all-gather.9.cloned.1.call-update) | async-done | bytes 2097168 | tf_op jit(solution)/shard_map/all_gather | solution.py:103
  297.9 7.3 %fusion.10 = (f32[64,128]{1,0:T(8,128)S(1)}, f32[64,128]{1,0:T(8,128)S(1)}, f32[64,128]{1,0:T(8,128)S(1)}, f32[64,128]{1,0:T(8,128)S(1)}) fusion(f32[8,8,64,128]{3,2,1,0:T(8,128)} %broadcast_multiply_fusion.18, f32[8,8,64,128]{3,2,1,0:T(8,128)} %broadcast_multiply_fusion.19, f32[64,64,128]{2,1,0:T(8,128)} %all-gather.9.cloned.1.call-done, ...), kind=kLoop, calls=%fused_computation.57 | loop fusion | flops 8355840 | bytes 19005696 | tf_op jit(solution)/shard_map/reduce_sum | solution.py:113
  316.8 1.7 copy-done.4
  318.5 5.6 fusion.79
  327.5 1.7 constant_dynamic-update-slice_fusion.243
  329.2 68.5 %all-reduce.47.cloned.1.call-done = f32[4,64,128]{2,0,1:T(4,128)} async-done(((f32[4,64,128]{2,0,1:T(4,128)}), f32[4,64,128]{2,0,1:T(4,128)}) %all-reduce.47.cloned.1.call-update) | async-done | bytes 131088 | tf_op jit(solution)/shard_map/psum | solution.py:81
  399.1 13.3 %broadcast_multiply_fusion.2 = (f32[2,64,8,8,128]{4,1,0,3,2:T(8,128)}, f32[2,64,8,8,128]{4,1,0,3,2:T(8,128)}, f32[2,8,8,128]{3,0,2,1:T(2,128)}, f32[2,64,8,8]{1,0,3,2:T(2,128)}) fusion(f32[2,64,8,128]{3,1,0,2:T(8,128)} %bitcast.326, f32[2,64,128]{2,1,0:T(8,128)} %multiply_bitcast_fusion, f32[2,64,128]{2,1,0:T(8,128)} %copy.308, f32[2,64,128]{2,1,0:T(8,128)S(1)} %copy.295, ...), kind=kLoop, calls=%fused_computation.61 | loop fusion | flops 29335552 | bytes 26804224 | tf_op jit(solution)/shard_map/transpose(jvp())/mul | solution.py:38
  413.3 9.2 %fusion = (f32[2,64,128]{2,1,0:T(8,128)S(1)}, f32[2,64,128]{2,1,0:T(8,128)}, f32[2,64,8,128]{3,1,0,2:T(8,128)}, f32[2,64,8,128]{3,1,0,2:T(8,128)}, f32[2,64,8,8]{1,0,3,2:T(2,128)}, /*index=5*/f32[2,64,8,8,128]{4,1,0,3,2:T(8,128)}) fusion(f32[2,64,8,8,128]{4,1,0,3,2:T(8,128)} %get-tuple-element.40, f32[2,64,8,8,128]{4,1,0,3,2:T(8,128)S(1)} %copy-done.5, ...), kind=kLoop, calls=%fused_computation.2 | loop fusion | flops 29057024 | bytes 27820032 | tf_op jit(solution)/shard_map/transpose(jvp())/reduce_sum | solution.py:70
  426.5 2.1 broadcast_multiply_fusion.10
  439.7 3.3 broadcast_multiply_fusion.8
  443.0 3.4 broadcast_multiply_fusion.9
  450.5 1.9 fusion.58
  452.4 18.2 %all-gather.11.cloned.1.call-done = f32[64,64,128]{2,1,0:T(8,128)} async-done(((f32[4,64,128]{2,1,0:T(8,128)}), f32[64,64,128]{2,1,0:T(8,128)}) %all-gather.11.cloned.1.call-update) | async-done | bytes 2097168 | tf_op jit(solution)/shard_map/all_gather | solution.py:103
  470.6 6.7 %fusion.6 = (f32[64,128]{1,0:T(8,128)S(1)}, f32[64,128]{1,0:T(8,128)S(1)}, f32[64,128]{1,0:T(8,128)S(1)}, f32[64,128]{1,0:T(8,128)S(1)}) fusion(f32[8,8,64,128]{3,2,1,0:T(8,128)S(1)} %broadcast_multiply_fusion.10, f32[8,8,64,128]{3,2,1,0:T(8,128)} %broadcast_multiply_fusion.11, f32[64,64,128]{2,1,0:T(8,128)} %all-gather.11.cloned.1.call-done, ...), kind=kLoop, calls=%fused_computation.45 | loop fusion | flops 8355840 | bytes 19005696 | tf_op jit(solution)/shard_map/reduce_sum | solution.py:113
  488.5 1.9 multiply_reduce_fusion
  492.5 72.3 %all-reduce.49.cloned.1.call-done = (f32[4,64,128]{2,0,1:T(4,128)}, f32[4,64,128]{2,0,1:T(4,128)}) async-done(((f32[4,64,128]{2,0,1:T(4,128)}, f32[4,64,128]{2,0,1:T(4,128)}), (f32[4,64,128]{2,0,1:T(4,128)}, f32[4,64,128]{2,0,1:T(4,128)})) %all-reduce.49.cloned.1.call-update) | async-done | bytes 262160 | tf_op jit(solution)/shard_map/psum | solution.py:140
  (762 shorter events, 163.0 us)
Async XLA Ops:
  7.2 69.8 %all-gather.5.cloned.1.call-start = ((), (), s32[]{:S(2)}) async-start(), calls=%async_computation | async-start | bytes 2228224 | tf_op jit(solution)/shard_map/all_gather | solution.py:87
  12.2 18.4 %copy-start.183 = (pred[2]{0:T(512)(128)(4,1)}, pred[2]{0:T(512)(128)(4,1)S(1)}, u32[]{:S(2)}) copy-start(pred[2]{0:T(512)(128)(4,1)S(1)} %iota_compare_fusion.15) | copy-start | bytes 10
  14.6 29.5 %copy-start.35 = (f32[2,64,8,1,128]{4,1,0,3,2:T(8,128)}, f32[2,64,8,1,128]{4,1,0,3,2:T(8,128)S(1)}, u32[]{:S(2)}) copy-start(f32[2,64,8,1,128]{4,1,0,3,2:T(8,128)S(1)} %get-tuple-element.226) | copy-start | bytes 1572868
  25.1 12.0 %copy-start.93 = (f32[2,64,1,1,128]{4,1,0,3,2:T(8,128)}, f32[2,64,1,1,128]{4,1,0,3,2:T(8,128)S(1)}, u32[]{:S(2)}) copy-start(f32[2,64,1,1,128]{4,1,0,3,2:T(8,128)S(1)} %get-tuple-element.217) | copy-start | bytes 196612
  25.4 57.6 %copy-start.47 = (f32[2,64,8,1,128]{4,1,0,3,2:T(8,128)}, f32[2,64,8,1,128]{4,1,0,3,2:T(8,128)S(1)}, u32[]{:S(2)}) copy-start(f32[2,64,8,1,128]{4,1,0,3,2:T(8,128)S(1)} %get-tuple-element.325) | copy-start | bytes 1572868
  26.9 134.0 %all-reduce.45.cloned.1.call-start = ((), (), s32[]{:S(2)}) async-start(), calls=%async_computation.1 | async-start | bytes 262144 | tf_op jit(solution)/shard_map/psum | solution.py:140
  27.1 22.9 %copy-start.185 = (pred[2,2]{1,0:T(4,128)(4,1)}, pred[2,2]{1,0:T(4,128)(4,1)S(1)}, u32[]{:S(2)}) copy-start(pred[2,2]{1,0:T(4,128)(4,1)S(1)} %get-tuple-element.394) | copy-start | bytes 16
  27.1 22.9 %copy-start.187 = (pred[2,2]{1,0:T(4,128)(4,1)}, pred[2,2]{1,0:T(4,128)(4,1)S(1)}, u32[]{:S(2)}) copy-start(pred[2,2]{1,0:T(4,128)(4,1)S(1)} %get-tuple-element.395) | copy-start | bytes 16
  37.1 9.9 %copy-start.49 = (f32[2,64,8,1,128]{4,1,0,3,2:T(8,128)}, f32[2,64,8,1,128]{4,1,0,3,2:T(8,128)S(1)}, u32[]{:S(2)}) copy-start(f32[2,64,8,1,128]{4,1,0,3,2:T(8,128)S(1)} %constant_dynamic-update-slice_fusion.24) | copy-start | bytes 1572868
  50.0 31.9 %copy-start.101 = (f32[2,2,64,128]{3,2,1,0:T(8,128)}, f32[2,2,64,128]{3,2,1,0:T(8,128)S(1)}, u32[]{:S(2)}) copy-start(f32[2,2,64,128]{3,2,1,0:T(8,128)S(1)} %get-tuple-element.390) | copy-start | bytes 393220
  50.0 32.9 %copy-start.81 = (f32[2,64,128]{2,1,0:T(8,128)}, f32[2,64,128]{2,1,0:T(8,128)S(1)}, u32[]{:S(2)}) copy-start(f32[2,64,128]{2,1,0:T(8,128)S(1)} %get-tuple-element.391) | copy-start | bytes 196612
  88.5 136.7 %all-gather.7.cloned.1.call-start = ((), (), s32[]{:S(2)}) async-start(), calls=%async_computation.2 | async-start | bytes 2228224 | tf_op jit(solution)/shard_map/all_gather | solution.py:87
  116.0 46.8 %copy-start.82 = (f32[2,64,128]{2,1,0:T(8,128)S(1)}, f32[2,64,128]{2,1,0:T(8,128)}, u32[]{:S(2)}) copy-start(f32[2,64,128]{2,1,0:T(8,128)} %copy-done.81) | copy-start | bytes 196612
  116.0 46.8 %copy-start.86 = (f32[2,64,128]{2,1,0:T(8,128)S(1)}, f32[2,64,128]{2,1,0:T(8,128)}, u32[]{:S(2)}) copy-start(f32[2,64,128]{2,1,0:T(8,128)} %copy-done.85) | copy-start | bytes 196612
  116.0 46.8 %copy-start.118 = (pred[2,64,8,8]{1,0,3,2:T(4,128)(4,1)S(1)}, pred[2,64,8,8]{1,0,3,2:T(4,128)(4,1)}, u32[]{:S(2)}) copy-start(pred[2,64,8,8]{1,0,3,2:T(4,128)(4,1)} %copy-done.117) | copy-start | bytes 24580
  117.0 52.0 %copy-start.54 = (f32[8,1,64,128]{3,2,1,0:T(8,128)}, f32[8,1,64,128]{3,2,1,0:T(8,128)S(1)}, u32[]{:S(2)}) copy-start(f32[8,1,64,128]{3,2,1,0:T(8,128)S(1)} %get-tuple-element.258) | copy-start | bytes 786436
  120.8 48.3 %copy-start.156 = (f32[1,1,64,128]{3,2,1,0:T(8,128)}, f32[1,1,64,128]{3,2,1,0:T(8,128)S(1)}, u32[]{:S(2)}) copy-start(f32[1,1,64,128]{3,2,1,0:T(8,128)S(1)} %get-tuple-element.51) | copy-start | bytes 98308
  178.2 119.6 %all-gather.9.cloned.1.call-start = ((), (), s32[]{:S(2)}) async-start(), calls=%async_computation.3 | async-start | bytes 2228224 | tf_op jit(solution)/shard_map/all_gather | solution.py:103
  178.3 13.7 %copy-start.37 = (f32[2,64,8,1,128]{4,1,0,3,2:T(8,128)S(1)}, f32[2,64,8,1,128]{4,1,0,3,2:T(8,128)}, u32[]{:S(2)}) copy-start(f32[2,64,8,1,128]{4,1,0,3,2:T(8,128)} %get-tuple-element.253) | copy-start | bytes 1572868
  251.4 146.4 %all-reduce.47.cloned.1.call-start = ((), (), s32[]{:S(2)}) async-start(), calls=%async_computation.4 | async-start | bytes 262144 | tf_op jit(solution)/shard_map/psum | solution.py:81
  297.8 9.8 %copy-start.159 = (f32[1,1,64,128]{3,2,1,0:T(8,128)S(1)}, f32[1,1,64,128]{3,2,1,0:T(8,128)}, u32[]{:S(2)}) copy-start(f32[1,1,64,128]{3,2,1,0:T(8,128)} %copy-done.158) | copy-start | bytes 98308
  297.8 10.7 %copy-start.110 = (f32[2,4,64,128]{3,2,1,0:T(8,128)S(1)}, f32[2,4,64,128]{3,2,1,0:T(8,128)}, u32[]{:S(2)}) copy-start(f32[2,4,64,128]{3,2,1,0:T(8,128)} %get-tuple-element.386) | copy-start | bytes 786436
  297.8 10.7 %copy-start.181 = (pred[2,4]{1,0:T(4,128)(4,1)S(1)}, pred[2,4]{1,0:T(4,128)(4,1)}, u32[]{:S(2)}) copy-start(pred[2,4]{1,0:T(4,128)(4,1)} %copy-done.179) | copy-start | bytes 28
  297.8 10.8 %copy-start.60 = (f32[2,64,8,128]{3,1,0,2:T(8,128)S(1)}, f32[2,64,8,128]{3,1,0,2:T(8,128)}, u32[]{:S(2)}) copy-start(f32[2,64,8,128]{3,1,0,2:T(8,128)} %get-tuple-element.12) | copy-start | bytes 1572868
  297.8 10.8 %copy-start.100 = (f32[2,64,1,1,128]{4,1,0,3,2:T(8,128)S(1)}, f32[2,64,1,1,128]{4,1,0,3,2:T(8,128)}, u32[]{:S(2)}) copy-start(f32[2,64,1,1,128]{4,1,0,3,2:T(8,128)} %get-tuple-element.194) | copy-start | bytes 196612
  297.9 10.8 %copy-start.126 = (f32[2,64,128]{2,1,0:T(8,128)S(1)}, f32[2,64,128]{2,1,0:T(8,128)}, u32[]{:S(2)}) copy-start(f32[2,64,128]{2,1,0:T(8,128)} %fusion.31) | copy-start | bytes 196612
  297.9 11.1 %copy-start.18 = (f32[2,64,8,8,128]{4,1,0,3,2:T(8,128)S(1)}, f32[2,64,8,8,128]{4,1,0,3,2:T(8,128)}, u32[]{:S(2)}) copy-start(f32[2,64,8,8,128]{4,1,0,3,2:T(8,128)} %get-tuple-element.117) | copy-start | bytes 12582916
  318.5 80.5 %copy-start.48 = (f32[2,64,8,1,128]{4,1,0,3,2:T(8,128)S(1)}, f32[2,64,8,1,128]{4,1,0,3,2:T(8,128)}, u32[]{:S(2)}) copy-start(f32[2,64,8,1,128]{4,1,0,3,2:T(8,128)} %copy-done.47) | copy-start | bytes 1572868
  325.2 145.4 %all-gather.11.cloned.1.call-start = ((), (), s32[]{:S(2)}) async-start(), calls=%async_computation.5 | async-start | bytes 2228224 | tf_op jit(solution)/shard_map/all_gather | solution.py:103
  399.0 13.4 %copy-start.5 = (f32[2,64,8,8,128]{4,1,0,3,2:T(8,128)S(1)}, f32[2,64,8,8,128]{4,1,0,3,2:T(8,128)}, u32[]{:S(2)}) copy-start(f32[2,64,8,8,128]{4,1,0,3,2:T(8,128)} %get-tuple-element.208) | copy-start | bytes 12582916
  399.0 13.4 %copy-start.9 = (f32[2,64,8,8,128]{4,1,0,3,2:T(8,128)S(1)}, f32[2,64,8,8,128]{4,1,0,3,2:T(8,128)}, u32[]{:S(2)}) copy-start(f32[2,64,8,8,128]{4,1,0,3,2:T(8,128)} %copy-done.7) | copy-start | bytes 12582916
  399.0 13.4 %copy-start.10 = (f32[2,64,8,8,128]{4,1,0,3,2:T(8,128)S(1)}, f32[2,64,8,8,128]{4,1,0,3,2:T(8,128)}, u32[]{:S(2)}) copy-start(f32[2,64,8,8,128]{4,1,0,3,2:T(8,128)} %get-tuple-element.107) | copy-start | bytes 12582916
  399.0 14.3 %copy-start.21 = (f32[2,64,8,8,128]{4,1,0,3,2:T(8,128)S(1)}, f32[2,64,8,8,128]{4,1,0,3,2:T(8,128)}, u32[]{:S(2)}) copy-start(f32[2,64,8,8,128]{4,1,0,3,2:T(8,128)} %constant_dynamic-update-slice_fusion.16) | copy-start | bytes 12582916
  399.0 14.3 %copy-start.51 = (f32[2,64,8,1,128]{4,1,0,3,2:T(8,128)S(1)}, f32[2,64,8,1,128]{4,1,0,3,2:T(8,128)}, u32[]{:S(2)}) copy-start(f32[2,64,8,1,128]{4,1,0,3,2:T(8,128)} %copy-done.49) | copy-start | bytes 1572868
  399.0 14.3 %copy-start.84 = (f32[2,64,128]{2,1,0:T(8,128)S(1)}, f32[2,64,128]{2,1,0:T(8,128)}, u32[]{:S(2)}) copy-start(f32[2,64,128]{2,1,0:T(8,128)} %copy-done.81) | copy-start | bytes 196612
  399.0 14.3 %copy-start.88 = (f32[2,64,128]{2,1,0:T(8,128)S(1)}, f32[2,64,128]{2,1,0:T(8,128)}, u32[]{:S(2)}) copy-start(f32[2,64,128]{2,1,0:T(8,128)} %copy-done.85) | copy-start | bytes 196612
  399.0 14.3 %copy-start.121 = (f32[2,64,128]{2,1,0:T(8,128)S(1)}, f32[2,64,128]{2,1,0:T(8,128)}, u32[]{:S(2)}) copy-start(f32[2,64,128]{2,1,0:T(8,128)} %multiply_bitcast_fusion) | copy-start | bytes 196612
  399.1 14.2 %copy-start.125 = (f32[2,64,128]{2,1,0:T(8,128)S(1)}, f32[2,64,128]{2,1,0:T(8,128)}, u32[]{:S(2)}) copy-start(f32[2,64,128]{2,1,0:T(8,128)} %copy.308) | copy-start | bytes 196612
  423.6 141.2 %all-reduce.49.cloned.1.call-start = ((), (), s32[]{:S(2)}) async-start(), calls=%async_computation.6 | async-start | bytes 524288 | tf_op jit(solution)/shard_map/psum | solution.py:140
  443.0 27.6 %copy-start.178 = (pred[64]{0:T(512)(128)(4,1)S(1)}, pred[64]{0:T(512)(128)(4,1)}, u32[]{:S(2)}) copy-start(pred[64]{0:T(512)(128)(4,1)} %get-tuple-element.401) | copy-start | bytes 196
  452.4 27.6 %copy-start.59 = (f32[2,64,8,128]{3,1,0,2:T(8,128)S(1)}, f32[2,64,8,128]{3,1,0,2:T(8,128)}, u32[]{:S(2)}) copy-start(f32[2,64,8,128]{3,1,0,2:T(8,128)} %get-tuple-element.14) | copy-start | bytes 1572868
  452.4 27.6 %copy-start.112 = (f32[2,64,1,1,128]{4,1,0,3,2:T(8,128)S(1)}, f32[2,64,1,1,128]{4,1,0,3,2:T(8,128)}, u32[]{:S(2)}) copy-start(f32[2,64,1,1,128]{4,1,0,3,2:T(8,128)} %copy-done.111) | copy-start | bytes 196612
  470.6 9.2 %copy-start.151 = (f32[1,1,64,128]{3,2,1,0:T(8,128)S(1)}, f32[1,1,64,128]{3,2,1,0:T(8,128)}, u32[]{:S(2)}) copy-start(f32[1,1,64,128]{3,2,1,0:T(8,128)} %copy-done.150) | copy-start | bytes 98308
  470.6 9.2 %copy-start.109 = (f32[2,4,64,128]{3,2,1,0:T(8,128)S(1)}, f32[2,4,64,128]{3,2,1,0:T(8,128)}, u32[]{:S(2)}) copy-start(f32[2,4,64,128]{3,2,1,0:T(8,128)} %get-tuple-element.384) | copy-start | bytes 786436
  470.6 9.3 %copy-start.182 = (pred[2,4]{1,0:T(4,128)(4,1)S(1)}, pred[2,4]{1,0:T(4,128)(4,1)}, u32[]{:S(2)}) copy-start(pred[2,4]{1,0:T(4,128)(4,1)} %copy-done.179) | copy-start | bytes 28
  470.6 10.1 %copy-start.17 = (f32[2,64,8,8,128]{4,1,0,3,2:T(8,128)S(1)}, f32[2,64,8,8,128]{4,1,0,3,2:T(8,128)}, u32[]{:S(2)}) copy-start(f32[2,64,8,8,128]{4,1,0,3,2:T(8,128)} %get-tuple-element.39) | copy-start | bytes 12582916
  488.4 76.4 %copy-start.175 = (f32[4,64]{0,1:T(8,128)S(1)}, f32[4,64]{0,1:T(8,128)}, u32[]{:S(2)}) copy-start(f32[4,64]{0,1:T(8,128)} %copy.290) | copy-start | bytes 3076
  488.4 79.3 %copy-start.189 = (f32[256]{0:T(256)S(1)}, f32[256]{0:T(256)}, u32[]{:S(2)}) copy-start(f32[256]{0:T(256)} %reduce_sum.353) | copy-start | bytes 3076
  (150 other events, 455.3 us)
Sparse Core Ops, SparseCore 0:
  27.1 49.8 all-gather.4
  88.6 72.3 all-reduce.44
  178.3 46.7 all-gather.6
  251.5 46.2 all-gather.8
  325.3 72.4 all-reduce.46
  423.7 46.7 all-gather.10
  491.6 73.1 all-reduce.48
where the time goes:
time: 583 us; the launch traced here: 575 us
  waiting for transfers between devices  257 us (44%)
  other arithmetic  186 us (32%)
  local copies, waits for them, and re-layouts  103 us (18%)
  between operations  18.1 us (3%)
  matrix products  11 us (2%)
    psum x2, waiting for transfers between devices, body(): total = prior_dev[:, :, None] + lax.psum(column, 'chk')  107 us
    unnamed x483, local copies, waits for them, and re-layouts  85.7 us
    psum x1, waiting for transfers between devices, checks_total(): return lax.psum(values, 'chk')  68.5 us
    all_gather x2, waiting for transfers between devices, others_forward(): lax.all_gather(part, 'var', axis=0, tiled=True)  47.9 us
    unnamed x138, other arithmetic  41.4 us
    mul x10, other arithmetic, exclusive_both(): after = (inner_after * outer_after).reshape(shape)  34.6 us
    all_gather x2, waiting for transfers between devices, others_backward(): grad_piece = lax.all_gather(grads, 'var', axis=0, tiled=True)  32.7 us
    reduce_sum x2, other arithmetic, edge_messages(): product = sign_slot[:, :, None, :] * inner * others_slot[:, :, None, :]  17.7 us
  transfers between devices with their start and end apart: 7, of which 7 were waited for; matrix products, arithmetic and copies ran while one was open for 23% of the time, Pallas kernels for 0%

commit v1 on v0

--- a/solution.py
+++ b/solution.py
@@ -1,6 +1,8 @@
 import jax
 import jax.numpy as jnp
 from jax import lax
+from jax.experimental import pallas as pl
+from jax.experimental.pallas import tpu as pltpu
 from jax.sharding import PartitionSpec as P
 
 TILE = 64
@@ -117,7 +119,7 @@
     return jnp.stack(new_sums)
 
 
-def body(tile_bits, tile_pos, tile_count, edge_weight, syndrome, channel_prior, out_cot):
+def dense_body(tile_bits, tile_pos, tile_count, edge_weight, syndrome, channel_prior, out_cot):
     slot_total = tile_bits.shape[2]
     shots = syndrome.shape[1]
     check_blocks = syndrome.shape[0] // TILE
@@ -176,6 +178,468 @@
     )
 
 
+EDGES = 128
+STEPS = (1, 2, 4, 8)
+SPAN = 16
+NONE = 300.0
+FULL = 1000.0
+MESH_ID = pl.DeviceIdType.MESH
+F32 = jnp.float32
+BF16 = jnp.bfloat16
+
+
+def iota(shape, axis):
+    return lax.broadcasted_iota(jnp.int32, shape, axis)
+
+
+def take(values, index):
+    return jnp.take_along_axis(values, index, axis=1, mode="promise_in_bounds")
+
+
+def small_dot(left, right, dims):
+    return lax.dot_general(
+        left.astype(BF16), right.astype(BF16), (dims, ((), ())), preferred_element_type=F32
+    )
+
+
+def exact_dot(left, right, dims):
+    return lax.dot_general(
+        left, right, (dims, ((), ())), precision=EXACT, preferred_element_type=F32
+    )
+
+
+def edge_list(marks, key_rows, key_lanes):
+    ahead = (iota((128, 128), 0) < iota((128, 128), 1)).astype(F32)
+    within = small_dot(marks, ahead, ((1,), (0,)))
+    counts = small_dot(marks, jnp.ones((128, 128), F32), ((1,), (0,)))
+    lower = (key_lanes < key_rows).astype(F32)
+    start = small_dot(lower, counts, ((1,), (0,)))
+    place = iota((128, 128), 1).astype(F32)
+    row_hot = ((place >= start) & (place < start + counts)).astype(F32)
+    wanted = jnp.sum(row_hot * (place - start + 1.0), axis=0, keepdims=True)
+    ranks = small_dot(marks * (within + 1.0), row_hot, ((0,), (0,)))
+    lane_hot = ((ranks == wanted) & (wanted > 0.0)).astype(F32)
+    return row_hot, lane_hot, start + within, counts
+
+
+def unpack_cells(ref, kind):
+    return jnp.concatenate(
+        [ref[pl.ds(kind * 16 + j, 8, stride=64), :] for j in range(16)], axis=0
+    )
+
+
+def cells(values):
+    return [values[j * 8 : j * 8 + 8, :] for j in range(16)]
+
+
+def spread_rows(rows):
+    return jnp.broadcast_to(rows, (16, 8, 128)).reshape(128, 128)
+
+
+def pick(pair, index, upper):
+    return jnp.where(upper, take(pair[1], index), take(pair[0], index))
+
+
+def last_places(order):
+    out = []
+    for half in range(2):
+        key = (iota((128, 128), 1) + 128 * half).astype(F32)
+        place = jnp.zeros((128, 128), jnp.int32)
+        seen = jnp.full((128, 128), -1.0, F32)
+        for step in (64, 32, 16, 8, 4, 2, 1, 1):
+            value = take(order, place + (step - 1))
+            fits = value <= key
+            place = jnp.where(fits, place + step, place)
+            seen = jnp.where(fits, value, seen)
+        out.append((jnp.maximum(place - 1, 0), seen == key))
+    return out
+
+
+def back(values, step):
+    return pltpu.roll(values, step, 1)
+
+
+def fore(values, step):
+    return pltpu.roll(values, 128 - step, 1)
+
+
+def scan_products(values, same, shift):
+    saved = []
+    for step in STEPS:
+        before = jnp.where(same[step], shift(values, step), 1.0)
+        saved.append((before, values))
+        values = before * values
+    return values, jnp.where(same[1], shift(values, 1), 1.0), saved
+
+
+def scan_sums(sums, saved, same, shift):
+    for step, (before, values) in zip(STEPS, saved):
+        sums = jnp.where(same[step], shift(sums, step), 0.0) * values + before * sums
+    return sums, jnp.where(same[1], shift(sums, 1), 0.0)
+
+
+def cross_products(rows):
+    pieces = cells(rows)
+    first = [jnp.ones((8, 128), F32)]
+    for j in range(15):
+        first.append(first[-1] * pieces[j])
+    last = [jnp.ones((8, 128), F32)]
+    for j in range(15, 0, -1):
+        last.append(last[-1] * pieces[j])
+    last = last[::-1]
+    others = jnp.concatenate([a * b for a, b in zip(first, last)], axis=0)
+    return others, (pieces, first, last)
+
+
+def cross_sums(rows, saved):
+    pieces, first, last = saved
+    sums = cells(rows)
+    first_sum = [jnp.zeros((8, 128), F32)]
+    for j in range(15):
+        first_sum.append(first_sum[-1] * pieces[j] + first[j] * sums[j])
+    last_sum = [jnp.zeros((8, 128), F32)]
+    for j in range(15, 0, -1):
+        last_sum.append(last_sum[-1] * pieces[j] + last[j] * sums[j])
+    last_sum = last_sum[::-1]
+    return jnp.concatenate(
+        [first_sum[j] * last[j] + first[j] * last_sum[j] for j in range(16)], axis=0
+    )
+
+
+def sparse_kernel(
+    count_ref, pos_ref, bits_ref, weight_ref, syndrome_ref, prior_ref, cot_ref,
+    marg_ref, wgrad_ref, pgrad_ref, flag_ref,
+    raw_bits, raw_weight, row_hot_ref, lane_hot_ref, flip_ref,
+    sigma_out, sigma_in, cell_out, cell_in, block_out, block_in,
+    part_out, part_in, sum_out, sum_in, send_sem, recv_sem,
+):
+    i = lax.axis_index("chk")
+    j = lax.axis_index("var")
+    barrier = pltpu.get_barrier_semaphore()
+    for step in range(1, 16):
+        pl.semaphore_signal(
+            barrier, 1, device_id={"var": lax.rem(j + step, 16)}, device_id_type=MESH_ID
+        )
+    for step in range(1, 8):
+        pl.semaphore_signal(
+            barrier, 1, device_id={"chk": lax.rem(i + step, 8)}, device_id_type=MESH_ID
+        )
+
+    def send(axis, phase, source, target, rows):
+        me, size = (j, 16) if axis == "var" else (i, 8)
+        for step in range(1, size):
+            other = lax.rem(me + step, size)
+            pltpu.make_async_remote_copy(
+                src_ref=source(other),
+                dst_ref=target.at[pl.ds(pl.multiple_of(me * rows, 8), rows)],
+                send_sem=send_sem.at[phase],
+                recv_sem=recv_sem.at[phase],
+                device_id={axis: other},
+                device_id_type=MESH_ID,
+            ).start()
+
+    def await_all(sems, phase, target, rows, size):
+        whole = target.at[pl.ds(0, rows * (size - 1))]
+        pltpu.make_async_copy(whole, whole, sems.at[phase]).wait()
+
+    count = count_ref[0, 0]
+    live = (iota((2, 128), 0) < count).astype(F32)
+    for m in range(32):
+        lanes = pl.ds(m * 128, 128)
+        raw_bits[pl.ds(m * 2, 2), :] = bits_ref[0, 0, :, lanes].astype(F32) * live
+        raw_weight[pl.ds(m * 2, 2), :] = weight_ref[0, 0, :, lanes]
+    narrow = iota((64, 128), 1) < 64
+
+    def entries(ref):
+        value = ref[...]
+        low = jnp.where(narrow, value, 0.0)
+        high = jnp.where(narrow, pltpu.roll(value, 64, 1), 0.0)
+        return jnp.concatenate([low, high], axis=0)
+
+    marks = entries(raw_bits)
+    weights = entries(raw_weight)
+    p0, p1 = pos_ref[0, 0, 0, 0], pos_ref[0, 0, 1, 0]
+    q0, q1 = pos_ref[0, 0, 0, 1], pos_ref[0, 0, 1, 1]
+
+    def check_of(axis, shape=(128, 128)):
+        at = iota(shape, axis)
+        slot = at & 1
+        return jnp.where(slot == 0, p0, p1) * 64 + (at & 62) + (at >> 6), slot
+
+    def variable_of(axis):
+        at = iota((128, 128), axis)
+        slot = at >> 6
+        return jnp.where(slot == 0, q0, q1) * 64 + (at & 63), slot
+
+    def unique(pair):
+        return pair[0] * 2 + pair[1]
+
+    row_hot, lane_hot, place, counts = edge_list(
+        marks, unique(check_of(0)), unique(check_of(1))
+    )
+    row_hot_ref[...] = row_hot
+    lane_hot_ref[...] = lane_hot
+    checks, slots = check_of(1, (8, 128))
+    columns = jnp.where(slots == 0, q0, q1) * 64
+    table = jnp.where(
+        iota((8, 128), 0) == 0,
+        checks,
+        jnp.where(iota((8, 128), 0) == 1, columns, 1),
+    ).astype(F32)
+    looked = small_dot(table, row_hot, ((1,), (0,)))
+    present = looked[2:3, :] > 0.0
+    edge_check = jnp.where(present, looked[0:1, :], NONE)
+    total_edges = jnp.sum(counts[:, 0:1])
+    edge_check = jnp.where(total_edges > EDGES, FULL, edge_check)
+    within = iota((128, 128), 0).astype(F32)
+    edge_var = looked[1:2, :] + jnp.sum(lane_hot * within, axis=0, keepdims=True)
+    weight_at = exact_dot(weights, row_hot, ((0,), (0,)))
+    edge_weight = jnp.sum(weight_at * lane_hot, axis=0, keepdims=True)
+
+    def turned(values):
+        flipped = jnp.transpose(values)[0:64, :]
+        odd = (iota((64, 128), 1) & 1) == 1
+        return jnp.concatenate(
+            [jnp.where(odd, 0.0, flipped), jnp.where(odd, flipped, 0.0)], axis=0
+        )
+
+    marks_turned = turned(marks)
+    col_hot, down_hot, unused_place, unused_counts = edge_list(
+        marks_turned, unique(variable_of(0)), unique(variable_of(1))
+    )
+    place_at = small_dot(marks_turned * turned(place), col_hot, ((0,), (0,)))
+    order = jnp.sum(place_at * down_hot, axis=0, keepdims=True)
+
+    for half in range(2):
+        flip_ref[pl.ds(half * 128, 128), :] = jnp.transpose(
+            cot_ref[pl.ds(half * 128, 128), :]
+        )
+    shots = [
+        flip_ref[pl.ds(pl.multiple_of(half * 128 + i * 16, 16), 16), :] for half in range(2)
+    ]
+    prior_low = prior_ref[pl.ds(0, 128)].reshape(1, 128)
+    prior_high = prior_ref[pl.ds(128, 128)].reshape(1, 128)
+    fixed = jnp.concatenate(
+        [edge_weight, edge_check, edge_var, order, prior_low, prior_high], axis=0
+    )
+    for t in range(16):
+        cell_out[pl.ds(t * 8, 6), :] = fixed
+        cell_out[pl.ds(t * 8 + 6, 1), :] = shots[0][t : t + 1, :]
+        cell_out[pl.ds(t * 8 + 7, 1), :] = shots[1][t : t + 1, :]
+    own = pl.ds(pl.multiple_of(j * 8, 8), 8)
+    cell_in[own, :] = cell_out[own, :]
+    signs = 1.0 - 2.0 * syndrome_ref[...].astype(F32)
+    for half in range(2):
+        flip_ref[pl.ds(half * 128, 128), :] = jnp.transpose(
+            signs[half * 128 : half * 128 + 128, :]
+        )
+        sigma_out[pl.ds(half * 8, 8), :] = flip_ref[pl.ds(half * 128 + j, 8, stride=16), :]
+    own = pl.ds(pl.multiple_of(i * 16, 16), 16)
+    sigma_in[own, :] = sigma_out[...]
+
+    pl.semaphore_wait(barrier, 22)
+    send("var", 0, lambda t: cell_out.at[pl.ds(pl.multiple_of(t * 8, 8), 8)], cell_in, 8)
+    send("chk", 1, lambda t: sigma_out, sigma_in, 16)
+    await_all(recv_sem, 0, cell_in, 8, 16)
+    for kind in range(4):
+        block_out[pl.ds(kind * 16, 16), :] = cell_in[pl.ds(kind, 16, stride=8), :]
+    own = pl.ds(pl.multiple_of(i * 64, 64), 64)
+    block_in[own, :] = block_out[...]
+    send("chk", 2, lambda t: block_out, block_in, 64)
+    await_all(recv_sem, 1, sigma_in, 16, 8)
+
+    def column_rows(kind):
+        return cell_in[pl.ds(kind, 16, stride=8), :].reshape(16, 1, 128)
+
+    prior = (column_rows(4), column_rows(5))
+    cot = (column_rows(6), column_rows(7))
+    sigma = [
+        jnp.concatenate([sigma_in[pl.ds(half * 8 + i, 8, stride=16), :]] * 16, axis=0)
+        for half in range(2)
+    ]
+    await_all(recv_sem, 2, block_in, 64, 8)
+
+    weight = unpack_cells(block_in, 0)
+    check = unpack_cells(block_in, 1)
+    variable = unpack_cells(block_in, 2).astype(jnp.int32)
+    order = unpack_cells(block_in, 3).astype(jnp.int32)
+    valid = check < 256.0
+    check_index = jnp.minimum(check, 255.0).astype(jnp.int32)
+    check_upper = check_index >= 128
+    check_index = check_index & 127
+    var_upper = variable >= 128
+    var_index = variable & 127
+    by_var = jnp.where(valid, take(variable.astype(F32), order), NONE)
+    bad = (
+        (check > 500.0)
+        | (valid & (check == back(check, SPAN)))
+        | (valid & (by_var == back(by_var, SPAN)))
+    )
+    flag_ref[0, 0] = jnp.max(bad.astype(F32))
+    same_back = {step: check == back(check, step) for step in STEPS}
+    same_fore = {step: check == fore(check, step) for step in STEPS}
+    same_var = {step: by_var == back(by_var, step) for step in STEPS}
+    check_last = last_places(check)
+    var_last = last_places(by_var)
+    sign = pick(sigma, check_index, check_upper)
+
+    def to_edges(rows):
+        return pick([spread_rows(rows[0]), spread_rows(rows[1])], var_index, var_upper)
+
+    def to_variables(values):
+        values = take(values, order)
+        for step in STEPS:
+            values = values + jnp.where(same_var[step], back(values, step), 0.0)
+        return [
+            jnp.sum(
+                jnp.where(found, take(values, place), 0.0).reshape(16, 8, 128),
+                axis=1,
+                keepdims=True,
+            )
+            for place, found in var_last
+        ]
+
+    def exchange(messages):
+        halves = jnp.where(valid, jnp.tanh(0.5 * messages), 1.0)
+        ahead, before, saved_back = scan_products(halves, same_back, back)
+        unused, after, saved_fore = scan_products(halves, same_fore, fore)
+        others, saved_cross = [], []
+        for place, found in check_last:
+            other, kept = cross_products(jnp.where(found, take(ahead, place), 1.0))
+            others.append(other)
+            saved_cross.append(kept)
+        outside = pick(others, check_index, check_upper)
+        inner = before * after
+        damped = (DAMP * sign) * (inner * outside)
+        level = jnp.log((1.0 + damped) / (1.0 - damped))
+        saved = (halves, before, after, inner, outside, damped, saved_back, saved_fore, saved_cross)
+        return level, saved
+
+    def exchange_grad(grad_update, saved):
+        halves, before, after, inner, outside, damped, saved_back, saved_fore, saved_cross = saved
+        leaf = grad_update * weight * sign * ((2.0 * DAMP) / (1.0 - damped * damped))
+        whole, before_sum = scan_sums(leaf, saved_back, same_back, back)
+        unused, after_sum = scan_sums(leaf, saved_fore, same_fore, fore)
+        outer = [
+            cross_sums(jnp.where(found, take(whole, place), 0.0), kept)
+            for (place, found), kept in zip(check_last, saved_cross)
+        ]
+        outside_sum = pick(outer, check_index, check_upper)
+        grad = (before_sum * after + before * after_sum) * outside + inner * outside_sum
+        return grad * (0.5 * (1.0 - halves * halves))
+
+    level_one, saved_one = exchange(to_edges(prior))
+    update = weight * level_one
+    total = [a + b for a, b in zip(prior, to_variables(update))]
+    level_two, saved_two = exchange(to_edges(total) - update)
+    marginal = [a + b for a, b in zip(prior, to_variables(weight * level_two))]
+    edge_cot = to_edges(cot)
+    grad_message = exchange_grad(edge_cot, saved_two)
+    grad_total = to_variables(grad_message)
+    grad_update = to_edges(grad_total) - grad_message
+    grad_weight = edge_cot * level_two + grad_update * level_one
+    grad_first = to_variables(exchange_grad(grad_update, saved_one))
+    grad_prior = [a + b + c for a, b, c in zip(cot, grad_total, grad_first)]
+
+    for half in range(2):
+        for t in range(16):
+            part_out[pl.ds(t * 16 + half, 1), :] = marginal[half][t]
+            part_out[pl.ds(t * 16 + 2 + half, 1), :] = grad_prior[half][t]
+    for t in range(16):
+        part_out[pl.ds(t * 16 + 8, 8), :] = grad_weight[t * 8 : t * 8 + 8, :]
+    own = pl.ds(pl.multiple_of(j * 16, 16), 16)
+    part_in[own, :] = part_out[own, :]
+    send("var", 3, lambda t: part_out.at[pl.ds(pl.multiple_of(t * 16, 16), 16)], part_in, 16)
+    await_all(recv_sem, 3, part_in, 16, 16)
+    for half in range(2):
+        sum_out[pl.ds(half * 16, 16), :] = part_in[pl.ds(half, 16, stride=16), :]
+    weight_sum = part_in[8:16, :]
+    for t in range(1, 16):
+        weight_sum = weight_sum + part_in[pl.ds(t * 16 + 8, 8), :]
+    sum_out[pl.ds(32, 8), :] = weight_sum
+    for half in range(2):
+        sum_out[pl.ds(40 + half, 1), :] = jnp.sum(
+            part_in[pl.ds(2 + half, 16, stride=16), :], axis=0, keepdims=True
+        )
+    own = pl.ds(pl.multiple_of(i * 48, 16), 48)
+    sum_in[own, :] = sum_out[...]
+    send("chk", 4, lambda t: sum_out, sum_in, 48)
+    await_all(recv_sem, 4, sum_in, 48, 8)
+    for half in range(2):
+        rows = jnp.concatenate(
+            [sum_in[pl.ds(t * 48 + half * 16, 16), :] for t in range(8)], axis=0
+        )
+        marg_ref[pl.ds(half * 128, 128), :] = jnp.transpose(rows)
+        pgrad_ref[pl.ds(half * 128, 128)] = jnp.sum(
+            sum_in[pl.ds(40 + half, 8, stride=48), :], axis=0
+        )
+    edge_grad = jnp.sum(sum_in[pl.ds(32 + i, 8, stride=48), :], axis=0, keepdims=True)
+    spread = row_hot_ref[...] * edge_grad
+    hot = lane_hot_ref[0:64, :]
+    nothing = jnp.zeros((64, 128), F32)
+    dense = exact_dot(
+        spread[0:64, :], jnp.concatenate([hot, nothing], axis=0), ((1,), (1,))
+    ) + exact_dot(spread[64:128, :], jnp.concatenate([nothing, hot], axis=0), ((1,), (1,)))
+    for m in range(32):
+        wgrad_ref[0, 0, :, pl.ds(m * 128, 128)] = dense[m * 2 : m * 2 + 2, :]
+
+    await_all(send_sem, 0, cell_out, 8, 16)
+    await_all(send_sem, 1, sigma_in, 16, 8)
+    await_all(send_sem, 2, block_in, 64, 8)
+    await_all(send_sem, 3, part_out, 16, 16)
+    await_all(send_sem, 4, sum_in, 48, 8)
+
+
+def sparse_body(tile_bits, tile_pos, tile_count, edge_weight, syndrome, channel_prior, out_cot):
+    vmem = pl.BlockSpec(memory_space=pltpu.VMEM)
+    smem = pl.BlockSpec(memory_space=pltpu.SMEM)
+    shape = jax.ShapeDtypeStruct
+    return pl.pallas_call(
+        sparse_kernel,
+        out_shape=(
+            shape(out_cot.shape, F32),
+            shape(edge_weight.shape, F32),
+            shape(channel_prior.shape, F32),
+            shape((1, 1), F32),
+        ),
+        in_specs=[smem, smem] + [vmem] * 5,
+        out_specs=(vmem, vmem, vmem, smem),
+        scratch_shapes=[
+            pltpu.VMEM((64, 128), F32),
+            pltpu.VMEM((64, 128), F32),
+            pltpu.VMEM((128, 128), F32),
+            pltpu.VMEM((128, 128), F32),
+            pltpu.VMEM((256, 128), F32),
+            pltpu.VMEM((16, 128), F32),
+            pltpu.VMEM((128, 128), F32),
+            pltpu.VMEM((128, 128), F32),
+            pltpu.VMEM((128, 128), F32),
+            pltpu.VMEM((64, 128), F32),
+            pltpu.VMEM((512, 128), F32),
+            pltpu.VMEM((256, 128), F32),
+            pltpu.VMEM((256, 128), F32),
+            pltpu.VMEM((48, 128), F32),
+            pltpu.VMEM((384, 128), F32),
+            pltpu.SemaphoreType.DMA((5,)),
+            pltpu.SemaphoreType.DMA((5,)),
+        ],
+        compiler_params=pltpu.CompilerParams(
+            collective_id=0, has_side_effects=True, vmem_limit_bytes=48 << 20
+        ),
+    )(tile_count, tile_pos, tile_bits, edge_weight, syndrome, channel_prior, out_cot)
+
+
+def body(*arguments):
+    *results, flag = sparse_body(*arguments)
+    return lax.cond(
+        flag[0, 0] > 0.0,
+        lambda given, kept: dense_body(*given),
+        lambda given, kept: kept,
+        arguments,
+        tuple(results),
+    )
+
+
 def solution(mesh):
     placed = (
         P("chk", "var", None, None),

time: 583 us -> 57.4 us (0.10)
  the two profiles are of different devices: /device:TPU:0 before, /device:TPU:1 now
where the time goes in v1:
time: 57.4 us; the launch traced here: 57.1 us
  Pallas kernels  37.4 us (65%)
  between operations  15.3 us (27%)
  local copies, waits for them, and re-layouts  4.13 us (7%)
    pallas_call x1, Pallas kernels, sparse_body(): pl.pallas_call(sparse_kernel, out_shape=(shape(out_cot.shape, F32), shape...  37.4 us
    unnamed x3, local copies, waits for them, and re-layouts  4.13 us

profile of v1, /device:TPU:1, one launch (start us, length us, event | category | flops | bytes accessed | tf_op | source)
XLA Modules:
  0.0 57.1 jit_solution(12074936806219107048)
XLA Ops:
  7.8 37.4 %shard_map.100 = (f32[256,128]{1,0:T(8,128)}, f32[1,1,2,4096]{3,2,1,0:T(2,128)}, f32[256]{0:T(256)}, f32[1,1]{1,0:T(1,128)}) custom-call(s32[1,1]{1,0:T(1,128)S(6)} %copy.621.count_ref, s32[1,1,2,2]{3,2,1,0:T(2,128)} %pos_ref.1, s32[1,1,2,4096]{3,2,1,0:T(2,128)} %bits_ref.1, f32[1,1,2,4096]{3,2,1,0:T(2,128)} %weight_ref.1, s32[256,128]{1,0:T(8,128)} %syndrome_ref.1, ...), custom_call_target="tpu_custom_call" | custom-call | tf_op jit(solution)/shard_map/pallas_call | solution.py:597
  45.9 0.2 conditional.1
  46.1 1.6 %copy.622 = f32[256,128]{1,0:T(8,128)} copy(f32[256,128]{1,0:T(8,128)} %get-tuple-element.455) | data formatting | bytes 262144
  47.7 1.4 %copy.623 = f32[1,1,2,4096]{3,2,1,0:T(2,128)} copy(f32[1,1,2,4096]{3,2,1,0:T(2,128)} %get-tuple-element.456) | data formatting | bytes 65536
  49.1 1.2 %copy.624 = f32[256]{0:T(256)} copy(f32[256]{0:T(256)} %get-tuple-element.457) | data formatting | bytes 2048

commit v2 on v1

--- a/solution.py
+++ b/solution.py
@@ -79,14 +79,62 @@
     return jnp.einsum("kv,kcs->vcs", col_hot, jnp.sum(values, axis=1), precision=EXACT)
 
 
+def gather_all(values, axis):
+    shape = values.shape
+    rows = values.size // shape[-1]
+    size = lax.axis_size(axis)
+
+    def kernel(given, out, send_sem, recv_sem):
+        me = lax.axis_index(axis)
+        barrier = pltpu.get_barrier_semaphore()
+        for step in range(1, size):
+            pl.semaphore_signal(
+                barrier,
+                1,
+                device_id={axis: lax.rem(me + step, size)},
+                device_id_type=pl.DeviceIdType.MESH,
+            )
+        pl.semaphore_wait(barrier, size - 1)
+        own = out.at[me]
+        for step in range(1, size):
+            pltpu.make_async_remote_copy(
+                src_ref=given,
+                dst_ref=own,
+                send_sem=send_sem,
+                recv_sem=recv_sem,
+                device_id={axis: lax.rem(me + step, size)},
+                device_id_type=pl.DeviceIdType.MESH,
+            ).start()
+        own[...] = given[...]
+        whole = out.at[pl.ds(0, size - 1)]
+        pltpu.make_async_copy(whole, whole, recv_sem).wait()
+        pltpu.make_async_copy(whole, whole, send_sem).wait()
+
+    gathered = pl.pallas_call(
+        kernel,
+        out_shape=jax.ShapeDtypeStruct((size, rows, shape[-1]), values.dtype),
+        in_specs=[pl.BlockSpec(memory_space=pltpu.VMEM)],
+        out_specs=pl.BlockSpec(memory_space=pltpu.VMEM),
+        scratch_shapes=[pltpu.SemaphoreType.DMA, pltpu.SemaphoreType.DMA],
+        compiler_params=pltpu.CompilerParams(
+            collective_id=1 if axis == "chk" else 2, has_side_effects=True
+        ),
+    )(values.reshape(rows, shape[-1]))
+    return gathered.reshape((size,) + shape)
+
+
+def gather_blocks(values):
+    return gather_all(values, "var").reshape((-1,) + values.shape[1:])
+
+
 def checks_total(values):
-    return lax.psum(values, "chk")
+    return jnp.sum(gather_all(values, "chk"), axis=0)
 
 
 def others_forward(rows, check_blocks):
     own = lax.axis_index("var")
     carry = jnp.ones_like(rows)
-    piece = jax.tree.map(lambda part: lax.all_gather(part, "var", axis=0, tiled=True), rows)
+    piece = gather_blocks(rows)
     indices = jnp.arange(piece.shape[0], dtype=jnp.int32)
     keep = indices // check_blocks != own
     parts = []
@@ -101,8 +149,8 @@
     own = lax.axis_index("var")
     kept_products = jnp.ones_like(rows)
     kept_sums = jnp.zeros_like(rows)
-    row_piece = lax.all_gather(rows, "var", axis=0, tiled=True)
-    grad_piece = lax.all_gather(grads, "var", axis=0, tiled=True)
+    row_piece = gather_blocks(rows)
+    grad_piece = gather_blocks(grads)
     indices = jnp.arange(row_piece.shape[0], dtype=jnp.int32)
     keep = indices // check_blocks != own
     new_products = []
@@ -139,7 +187,7 @@
         inner, rows = row_products(messages, edge, row_hot, same_row)
         others, kept = others_forward(rows, check_blocks)
         update, column = edge_messages(inner, others, weight, sign_slot, edge, row_hot, col_hot)
-        total = prior_dev[:, :, None] + lax.psum(column, "chk")
+        total = prior_dev[:, :, None] + checks_total(column)
         saved.append((messages, inner, rows, others, kept))
         if step + 1 < ITERS:
             spread = jnp.einsum("kv,vcs->kcs", col_hot, total, precision=EXACT)
@@ -308,10 +356,10 @@
 
 def sparse_kernel(
     count_ref, pos_ref, bits_ref, weight_ref, syndrome_ref, prior_ref, cot_ref,
-    marg_ref, wgrad_ref, pgrad_ref, flag_ref,
-    raw_bits, raw_weight, row_hot_ref, lane_hot_ref, flip_ref,
+    sum_in, row_hot_ref, lane_hot_ref, flag_ref,
+    raw_bits, raw_weight, flip_ref,
     sigma_out, sigma_in, cell_out, cell_in, block_out, block_in,
-    part_out, part_in, sum_out, sum_in, send_sem, recv_sem,
+    part_out, part_in, sum_out, send_sem, recv_sem,
 ):
     i = lax.axis_index("chk")
     j = lax.axis_index("var")
@@ -565,6 +613,15 @@
     sum_in[own, :] = sum_out[...]
     send("chk", 4, lambda t: sum_out, sum_in, 48)
     await_all(recv_sem, 4, sum_in, 48, 8)
+    await_all(send_sem, 0, cell_out, 8, 16)
+    await_all(send_sem, 1, sigma_in, 16, 8)
+    await_all(send_sem, 2, block_in, 64, 8)
+    await_all(send_sem, 3, part_out, 16, 16)
+    await_all(send_sem, 4, sum_in, 48, 8)
+
+
+def finish_kernel(sum_in, row_hot_ref, lane_hot_ref, marg_ref, wgrad_ref, pgrad_ref):
+    i = lax.axis_index("chk")
     for half in range(2):
         rows = jnp.concatenate(
             [sum_in[pl.ds(t * 48 + half * 16, 16), :] for t in range(8)], axis=0
@@ -583,32 +640,26 @@
     for m in range(32):
         wgrad_ref[0, 0, :, pl.ds(m * 128, 128)] = dense[m * 2 : m * 2 + 2, :]
 
-    await_all(send_sem, 0, cell_out, 8, 16)
-    await_all(send_sem, 1, sigma_in, 16, 8)
-    await_all(send_sem, 2, block_in, 64, 8)
-    await_all(send_sem, 3, part_out, 16, 16)
-    await_all(send_sem, 4, sum_in, 48, 8)
-
-
-def sparse_body(tile_bits, tile_pos, tile_count, edge_weight, syndrome, channel_prior, out_cot):
-    vmem = pl.BlockSpec(memory_space=pltpu.VMEM)
-    smem = pl.BlockSpec(memory_space=pltpu.SMEM)
+
+VMEM_SPEC = pl.BlockSpec(memory_space=pltpu.VMEM)
+SMEM_SPEC = pl.BlockSpec(memory_space=pltpu.SMEM)
+
+
+def sparse_parts(tile_bits, tile_pos, tile_count, edge_weight, syndrome, channel_prior, out_cot):
     shape = jax.ShapeDtypeStruct
     return pl.pallas_call(
         sparse_kernel,
         out_shape=(
-            shape(out_cot.shape, F32),
-            shape(edge_weight.shape, F32),
-            shape(channel_prior.shape, F32),
+            shape((384, 128), F32),
+            shape((128, 128), F32),
+            shape((128, 128), F32),
             shape((1, 1), F32),
         ),
-        in_specs=[smem, smem] + [vmem] * 5,
-        out_specs=(vmem, vmem, vmem, smem),
+        in_specs=[SMEM_SPEC] * 2 + [VMEM_SPEC] * 5,
+        out_specs=(VMEM_SPEC, VMEM_SPEC, VMEM_SPEC, SMEM_SPEC),
         scratch_shapes=[
             pltpu.VMEM((64, 128), F32),
             pltpu.VMEM((64, 128), F32),
-            pltpu.VMEM((128, 128), F32),
-            pltpu.VMEM((128, 128), F32),
             pltpu.VMEM((256, 128), F32),
             pltpu.VMEM((16, 128), F32),
             pltpu.VMEM((128, 128), F32),
@@ -619,7 +670,6 @@
             pltpu.VMEM((256, 128), F32),
             pltpu.VMEM((256, 128), F32),
             pltpu.VMEM((48, 128), F32),
-            pltpu.VMEM((384, 128), F32),
             pltpu.SemaphoreType.DMA((5,)),
             pltpu.SemaphoreType.DMA((5,)),
         ],
@@ -629,14 +679,28 @@
     )(tile_count, tile_pos, tile_bits, edge_weight, syndrome, channel_prior, out_cot)
 
 
+def finish(parts, row_hot, lane_hot):
+    shape = jax.ShapeDtypeStruct
+    return pl.pallas_call(
+        finish_kernel,
+        out_shape=(
+            shape((256, 128), F32),
+            shape((1, 1, 2, 4096), F32),
+            shape((256,), F32),
+        ),
+        in_specs=[VMEM_SPEC] * 3,
+        out_specs=(VMEM_SPEC,) * 3,
+    )(parts, row_hot, lane_hot)
+
+
 def body(*arguments):
-    *results, flag = sparse_body(*arguments)
+    *parts, flag = sparse_parts(*arguments)
     return lax.cond(
         flag[0, 0] > 0.0,
         lambda given, kept: dense_body(*given),
-        lambda given, kept: kept,
+        lambda given, kept: tuple(finish(*kept)),
         arguments,
-        tuple(results),
+        tuple(parts),
     )
 
 

time: 57.4 us -> 40.6 us (0.71)
  between operations: 15.3 us -> 1.97 us
  local copies, waits for them, and re-layouts: 4.13 us -> 0.56 us
    unnamed x3 -> x2, local copies, waits for them, and re-layouts: 4.13 us -> 0.56 us
    pallas_call x1 -> x2, Pallas kernels: 37.4 us -> 37.9 us  [the longest x1 37 us: sparse_parts(): pl.pallas_call(sparse_kernel, out_shape=(shape((384, 128), F32), shape((1...]
where the time goes in v2:
time: 40.6 us; the launch traced here: 40.4 us
  Pallas kernels  37.9 us (93%)
  between operations  1.97 us (5%)
  local copies, waits for them, and re-layouts  0.56 us (1%)
    pallas_call x1, Pallas kernels, sparse_parts(): pl.pallas_call(sparse_kernel, out_shape=(shape((384, 128), F32), shape((1...  37 us
    pallas_call x1, Pallas kernels, finish(): pl.pallas_call(finish_kernel, out_shape=(shape((256, 128), F32), shape((1...  0.91 us

profile of v2, /device:TPU:1, one launch (start us, length us, event | category | flops | bytes accessed | tf_op | source)
XLA Modules:
  0.0 40.4 jit_solution(12999137416833966315)
XLA Ops:
  1.3 37.0 %shard_map.100 = (f32[384,128]{1,0:T(8,128)S(1)}, f32[128,128]{1,0:T(8,128)S(1)}, f32[128,128]{1,0:T(8,128)S(1)}, f32[1,1]{1,0:T(1,128)}) custom-call(s32[1,1]{1,0:T(1,128)S(6)} %copy.404.count_ref, s32[1,1,2,2]{3,2,1,0:T(2,128)} %pos_ref.1, s32[1,1,2,4096]{3,2,1,0:T(2,128)} %bits_ref.1, f32[1,1,2,4096]{3,2,1,0:T(2,128)} %weight_ref.1, ...), custom_call_target="tpu_custom_call" | custom-call | tf_op jit(solution)/shard_map/pallas_call | solution.py:650
  38.9 0.9 %conditional.1 = ((f32[256,128]{1,0:T(8,128)}, f32[1,1,2,4096]{3,2,1,0:T(2,128)}, f32[256]{0:T(256)S(1)})) conditional(s32[]{:T(128)} %bitcast.111, (f32[384,128]{1,0:T(8,128)S(1)}, f32[128,128]{1,0:T(8,128)S(1)}, f32[128,128]{1,0:T(8,128)S(1)}) %tuple.23, (f32[256]{0:T(256)}, s32[1,1,2,2]{3,2,1,0:T(2,128)}, s32[1,1]{1,0:T(1,128)}, ...), branch_computations={%region_0.0_spmd, %region_1.46_spmd} | conditional | flops 258632576 | bytes 1007619712 | solution.py:698
  38.9 0.9 %branch_0_fun.1 = (f32[256,128]{1,0:T(8,128)}, f32[1,1,2,4096]{3,2,1,0:T(2,128)}, f32[256]{0:T(256)S(1)}) custom-call(f32[384,128]{1,0:T(8,128)S(1)} %get-tuple-element.20.sum_in, f32[128,128]{1,0:T(8,128)S(1)} %get-tuple-element.21.row_hot_ref, f32[128,128]{1,0:T(8,128)S(1)} %get-tuple-element.22.lane_hot_ref), custom_call_target="tpu_custom_call" | custom-call | tf_op jit(solution)/shard_map/cond/branch_0_fun/pallas_call | solution.py:684
  39.9 0.0 copy-start.133
  39.9 0.6 %copy-done.133 = f32[256]{0:T(256)} copy-done((f32[256]{0:T(256)}, f32[256]{0:T(256)S(1)}, u32[]{:S(2)}) %copy-start.133) | copy-done | bytes 1048
Async XLA Ops:
  39.9 0.6 %copy-start.133 = (f32[256]{0:T(256)}, f32[256]{0:T(256)S(1)}, u32[]{:S(2)}) copy-start(f32[256]{0:T(256)S(1)} %get-tuple-element.458) | copy-start | bytes 3076

commit v3 on v2

--- a/solution.py
+++ b/solution.py
@@ -227,8 +227,11 @@
 
 
 EDGES = 128
-STEPS = (1, 2, 4, 8)
-SPAN = 16
+NEAR = (1, 2)
+FAR = (1, 4, 7)
+VAR_FAR = (3, 6, 9)
+CHECK_SPAN = 10
+VAR_SPAN = 12
 NONE = 300.0
 FULL = 1000.0
 MESH_ID = pl.DeviceIdType.MESH
@@ -268,12 +271,6 @@
     ranks = small_dot(marks * (within + 1.0), row_hot, ((0,), (0,)))
     lane_hot = ((ranks == wanted) & (wanted > 0.0)).astype(F32)
     return row_hot, lane_hot, start + within, counts
-
-
-def unpack_cells(ref, kind):
-    return jnp.concatenate(
-        [ref[pl.ds(kind * 16 + j, 8, stride=64), :] for j in range(16)], axis=0
-    )
 
 
 def cells(values):
@@ -312,18 +309,18 @@
 
 
 def scan_products(values, same, shift):
-    saved = []
-    for step in STEPS:
-        before = jnp.where(same[step], shift(values, step), 1.0)
-        saved.append((before, values))
-        values = before * values
-    return values, jnp.where(same[1], shift(values, 1), 1.0), saved
+    one, two = (jnp.where(same[step], shift(values, step), 1.0) for step in NEAR)
+    group = values * one * two
+    far = [jnp.where(same[step], shift(group, step), 1.0) for step in FAR]
+    return far[0] * far[1] * far[2], (values, one, two, far)
 
 
 def scan_sums(sums, saved, same, shift):
-    for step, (before, values) in zip(STEPS, saved):
-        sums = jnp.where(same[step], shift(sums, step), 0.0) * values + before * sums
-    return sums, jnp.where(same[1], shift(sums, 1), 0.0)
+    values, one, two, far = saved
+    one_sum, two_sum = (jnp.where(same[step], shift(sums, step), 0.0) for step in NEAR)
+    group = (sums * one + values * one_sum) * two + (values * one) * two_sum
+    a, b, c = (jnp.where(same[step], shift(group, step), 0.0) for step in FAR)
+    return (a * far[1] + far[0] * b) * far[2] + (far[0] * far[1]) * c
 
 
 def cross_products(rows):
@@ -355,12 +352,15 @@
 
 
 def sparse_kernel(
-    count_ref, pos_ref, bits_ref, weight_ref, syndrome_ref, prior_ref, cot_ref,
-    sum_in, row_hot_ref, lane_hot_ref, flag_ref,
-    raw_bits, raw_weight, flip_ref,
-    sigma_out, sigma_in, cell_out, cell_in, block_out, block_in,
-    part_out, part_in, sum_out, send_sem, recv_sem,
+    count_hbm, pos_hbm, bits_hbm, weight_hbm, syndrome_hbm, prior_hbm, cot_hbm,
+    marg_ref, wgrad_ref, pgrad_ref, flag_ref,
+    count_ref, pos_ref, bits_ref, weight_ref, syndrome_ref, prior_ref, cot_ref, load_sem,
+    raw_bits, raw_weight, row_hot_ref, lane_hot_ref, flip_ref,
+    cell_out, cell_in, prior_out, prior_in, sigma_out, sigma_in, cot_out, cot_in,
+    marg_out, marg_in, weight_out, weight_in, late_out, late_in,
+    size_1, size_2, size_4, entered, send_sem, recv_sem,
 ):
+    row_sizes = {1: size_1, 2: size_2, 4: size_4}
     i = lax.axis_index("chk")
     j = lax.axis_index("var")
     barrier = pltpu.get_barrier_semaphore()
@@ -372,24 +372,46 @@
         pl.semaphore_signal(
             barrier, 1, device_id={"chk": lax.rem(i + step, 8)}, device_id_type=MESH_ID
         )
-
-    def send(axis, phase, source, target, rows):
-        me, size = (j, 16) if axis == "var" else (i, 8)
-        for step in range(1, size):
-            other = lax.rem(me + step, size)
-            pltpu.make_async_remote_copy(
-                src_ref=source(other),
-                dst_ref=target.at[pl.ds(pl.multiple_of(me * rows, 8), rows)],
-                send_sem=send_sem.at[phase],
-                recv_sem=recv_sem.at[phase],
-                device_id={axis: other},
-                device_id_type=MESH_ID,
-            ).start()
-
-    def await_all(sems, phase, target, rows, size):
-        whole = target.at[pl.ds(0, rows * (size - 1))]
+    loads = [
+        pltpu.make_async_copy(given, held, load_sem.at[at])
+        for at, (given, held) in enumerate(
+            (
+                (count_hbm, count_ref),
+                (pos_hbm, pos_ref),
+                (bits_hbm, bits_ref),
+                (weight_hbm, weight_ref),
+                (prior_hbm, prior_ref),
+                (cot_hbm, cot_ref),
+                (syndrome_hbm, syndrome_ref),
+            )
+        )
+    ]
+    for load in loads:
+        load.start()
+
+    def send(phase, source, target, row, turn):
+        pltpu.make_async_remote_copy(
+            src_ref=source,
+            dst_ref=target.at[pl.ds(row, 1)],
+            send_sem=send_sem.at[phase],
+            recv_sem=recv_sem.at[phase],
+            device_id={
+                "chk": lax.bitwise_xor(i, turn // 16),
+                "var": lax.bitwise_xor(j, turn % 16),
+            },
+            device_id_type=MESH_ID,
+        ).start()
+
+    everyone = sorted(range(1, 128), key=lambda turn: -bin(turn).count("1"))
+    of_row = [turn for turn in everyone if turn < 16]
+    of_column = [turn for turn in everyone if turn % 16 == 0]
+
+    def wait_for(sems, phase, target, count):
+        whole = row_sizes[target.shape[1] // 128].at[pl.ds(0, count)]
         pltpu.make_async_copy(whole, whole, sems.at[phase]).wait()
 
+    for load in loads[0:4]:
+        load.wait()
     count = count_ref[0, 0]
     live = (iota((2, 128), 0) < count).astype(F32)
     for m in range(32):
@@ -444,6 +466,15 @@
     weight_at = exact_dot(weights, row_hot, ((0,), (0,)))
     edge_weight = jnp.sum(weight_at * lane_hot, axis=0, keepdims=True)
 
+    pl.semaphore_wait(barrier, 22)
+    for turn in of_column:
+        pl.semaphore_signal(
+            entered,
+            1,
+            device_id={"chk": lax.bitwise_xor(i, turn // 16)},
+            device_id_type=MESH_ID,
+        )
+
     def turned(values):
         flipped = jnp.transpose(values)[0:64, :]
         odd = (iota((64, 128), 1) & 1) == 1
@@ -458,59 +489,63 @@
     place_at = small_dot(marks_turned * turned(place), col_hot, ((0,), (0,)))
     order = jnp.sum(place_at * down_hot, axis=0, keepdims=True)
 
+    pl.semaphore_wait(entered, 7)
+
+    own_cell = j * 8 + i
+    shot = i * 16 + j
+    for kind, row in enumerate((edge_weight, edge_check, edge_var, order)):
+        cell_out[:, pl.ds(kind * 128, 128)] = row
+    loads[4].wait()
     for half in range(2):
-        flip_ref[pl.ds(half * 128, 128), :] = jnp.transpose(
-            cot_ref[pl.ds(half * 128, 128), :]
-        )
-    shots = [
-        flip_ref[pl.ds(pl.multiple_of(half * 128 + i * 16, 16), 16), :] for half in range(2)
-    ]
-    prior_low = prior_ref[pl.ds(0, 128)].reshape(1, 128)
-    prior_high = prior_ref[pl.ds(128, 128)].reshape(1, 128)
-    fixed = jnp.concatenate(
-        [edge_weight, edge_check, edge_var, order, prior_low, prior_high], axis=0
-    )
-    for t in range(16):
-        cell_out[pl.ds(t * 8, 6), :] = fixed
-        cell_out[pl.ds(t * 8 + 6, 1), :] = shots[0][t : t + 1, :]
-        cell_out[pl.ds(t * 8 + 7, 1), :] = shots[1][t : t + 1, :]
-    own = pl.ds(pl.multiple_of(j * 8, 8), 8)
-    cell_in[own, :] = cell_out[own, :]
+        lanes = pl.ds(half * 128, 128)
+        prior_out[:, lanes] = prior_ref[lanes].reshape(1, 128)
+    for turn in of_row:
+        send(1, prior_out, prior_in, j, turn)
+    for turn in everyone:
+        send(0, cell_out, cell_in, own_cell, turn)
+    cell_in[pl.ds(own_cell, 1), :] = cell_out[...]
+    prior_in[pl.ds(j, 1), :] = prior_out[...]
+    loads[6].wait()
     signs = 1.0 - 2.0 * syndrome_ref[...].astype(F32)
     for half in range(2):
-        flip_ref[pl.ds(half * 128, 128), :] = jnp.transpose(
-            signs[half * 128 : half * 128 + 128, :]
+        rows = pl.ds(half * 128, 128)
+        flip_ref[rows, :] = jnp.transpose(signs[half * 128 : half * 128 + 128, :])
+        sigma_out[:, rows] = flip_ref[pl.ds(half * 128 + j, 8, stride=16), :]
+    for turn in of_column:
+        other = lax.bitwise_xor(i, turn // 16)
+        send(2, sigma_out.at[pl.ds(other, 1)], sigma_in, i, turn)
+    sigma_in[pl.ds(i, 1), :] = sigma_out[pl.ds(i, 1), :]
+    loads[5].wait()
+    for half in range(2):
+        rows = pl.ds(half * 128, 128)
+        flip_ref[rows, :] = jnp.transpose(cot_ref[rows, :])
+        start = pl.multiple_of(half * 128 + i * 16, 16)
+        cot_out[:, rows] = flip_ref[pl.ds(start, 16), :]
+    for turn in of_row:
+        other = lax.bitwise_xor(j, turn)
+        send(3, cot_out.at[pl.ds(other, 1)], cot_in, j, turn)
+    cot_in[pl.ds(j, 1), :] = cot_out[pl.ds(j, 1), :]
+
+    def column_rows(ref):
+        return tuple(
+            ref[:, half * 128 : half * 128 + 128].reshape(16, 1, 128) for half in range(2)
         )
-        sigma_out[pl.ds(half * 8, 8), :] = flip_ref[pl.ds(half * 128 + j, 8, stride=16), :]
-    own = pl.ds(pl.multiple_of(i * 16, 16), 16)
-    sigma_in[own, :] = sigma_out[...]
-
-    pl.semaphore_wait(barrier, 22)
-    send("var", 0, lambda t: cell_out.at[pl.ds(pl.multiple_of(t * 8, 8), 8)], cell_in, 8)
-    send("chk", 1, lambda t: sigma_out, sigma_in, 16)
-    await_all(recv_sem, 0, cell_in, 8, 16)
-    for kind in range(4):
-        block_out[pl.ds(kind * 16, 16), :] = cell_in[pl.ds(kind, 16, stride=8), :]
-    own = pl.ds(pl.multiple_of(i * 64, 64), 64)
-    block_in[own, :] = block_out[...]
-    send("chk", 2, lambda t: block_out, block_in, 64)
-    await_all(recv_sem, 1, sigma_in, 16, 8)
-
-    def column_rows(kind):
-        return cell_in[pl.ds(kind, 16, stride=8), :].reshape(16, 1, 128)
-
-    prior = (column_rows(4), column_rows(5))
-    cot = (column_rows(6), column_rows(7))
+
+    wait_for(recv_sem, 1, prior_in, 15)
+    wait_for(recv_sem, 2, sigma_in, 7)
+    wait_for(recv_sem, 3, cot_in, 15)
+    prior = column_rows(prior_in)
+    cot = column_rows(cot_in)
     sigma = [
-        jnp.concatenate([sigma_in[pl.ds(half * 8 + i, 8, stride=16), :]] * 16, axis=0)
+        jnp.concatenate([sigma_in[:, half * 128 : half * 128 + 128]] * 16, axis=0)
         for half in range(2)
     ]
-    await_all(recv_sem, 2, block_in, 64, 8)
-
-    weight = unpack_cells(block_in, 0)
-    check = unpack_cells(block_in, 1)
-    variable = unpack_cells(block_in, 2).astype(jnp.int32)
-    order = unpack_cells(block_in, 3).astype(jnp.int32)
+    wait_for(recv_sem, 0, cell_in, 127)
+
+    weight = cell_in[:, 0:128]
+    check = cell_in[:, 128:256]
+    variable = cell_in[:, 256:384].astype(jnp.int32)
+    order = cell_in[:, 384:512].astype(jnp.int32)
     valid = check < 256.0
     check_index = jnp.minimum(check, 255.0).astype(jnp.int32)
     check_upper = check_index >= 128
@@ -520,13 +555,14 @@
     by_var = jnp.where(valid, take(variable.astype(F32), order), NONE)
     bad = (
         (check > 500.0)
-        | (valid & (check == back(check, SPAN)))
-        | (valid & (by_var == back(by_var, SPAN)))
+        | (valid & (check == back(check, CHECK_SPAN)))
+        | (valid & (by_var == back(by_var, VAR_SPAN)))
     )
     flag_ref[0, 0] = jnp.max(bad.astype(F32))
-    same_back = {step: check == back(check, step) for step in STEPS}
-    same_fore = {step: check == fore(check, step) for step in STEPS}
-    same_var = {step: by_var == back(by_var, step) for step in STEPS}
+    same_back = {step: check == back(check, step) for step in (1, 2, 4, 7)}
+    same_fore = {step: check == fore(check, step) for step in (1, 2, 4, 7)}
+    same_var = {step: by_var == back(by_var, step) for step in NEAR + VAR_FAR}
+    orders = {step: back(order, step) for step in NEAR}
     check_last = last_places(check)
     var_last = last_places(by_var)
     sign = pick(sigma, check_index, check_upper)
@@ -535,9 +571,12 @@
         return pick([spread_rows(rows[0]), spread_rows(rows[1])], var_index, var_upper)
 
     def to_variables(values):
-        values = take(values, order)
-        for step in STEPS:
-            values = values + jnp.where(same_var[step], back(values, step), 0.0)
+        group = take(values, order)
+        for step in NEAR:
+            group = group + jnp.where(same_var[step], take(values, orders[step]), 0.0)
+        values = group
+        for step in VAR_FAR:
+            values = values + jnp.where(same_var[step], back(group, step), 0.0)
         return [
             jnp.sum(
                 jnp.where(found, take(values, place), 0.0).reshape(16, 8, 128),
@@ -549,8 +588,9 @@
 
     def exchange(messages):
         halves = jnp.where(valid, jnp.tanh(0.5 * messages), 1.0)
-        ahead, before, saved_back = scan_products(halves, same_back, back)
-        unused, after, saved_fore = scan_products(halves, same_fore, fore)
+        before, saved_back = scan_products(halves, same_back, back)
+        after, saved_fore = scan_products(halves, same_fore, fore)
+        ahead = halves * before
         others, saved_cross = [], []
         for place, found in check_last:
             other, kept = cross_products(jnp.where(found, take(ahead, place), 1.0))
@@ -566,8 +606,9 @@
     def exchange_grad(grad_update, saved):
         halves, before, after, inner, outside, damped, saved_back, saved_fore, saved_cross = saved
         leaf = grad_update * weight * sign * ((2.0 * DAMP) / (1.0 - damped * damped))
-        whole, before_sum = scan_sums(leaf, saved_back, same_back, back)
-        unused, after_sum = scan_sums(leaf, saved_fore, same_fore, fore)
+        before_sum = scan_sums(leaf, saved_back, same_back, back)
+        after_sum = scan_sums(leaf, saved_fore, same_fore, fore)
+        whole = leaf * before + halves * before_sum
         outer = [
             cross_sums(jnp.where(found, take(whole, place), 0.0), kept)
             for (place, found), kept in zip(check_last, saved_cross)
@@ -581,56 +622,41 @@
     total = [a + b for a, b in zip(prior, to_variables(update))]
     level_two, saved_two = exchange(to_edges(total) - update)
     marginal = [a + b for a, b in zip(prior, to_variables(weight * level_two))]
+    for half in range(2):
+        for t in range(16):
+            marg_out[pl.ds(t, 1), pl.ds(half * 128, 128)] = marginal[half][t]
+    for turn in everyone:
+        other = lax.bitwise_xor(j, turn % 16)
+        send(4, marg_out.at[pl.ds(other, 1)], marg_in, shot, turn)
+    marg_in[pl.ds(shot, 1), :] = marg_out[pl.ds(j, 1), :]
     edge_cot = to_edges(cot)
     grad_message = exchange_grad(edge_cot, saved_two)
     grad_total = to_variables(grad_message)
     grad_update = to_edges(grad_total) - grad_message
     grad_weight = edge_cot * level_two + grad_update * level_one
+    weight_out[...] = grad_weight
+    for turn in everyone:
+        other = lax.bitwise_xor(j, turn % 16) * 8 + lax.bitwise_xor(i, turn // 16)
+        send(5, weight_out.at[pl.ds(other, 1)], weight_in, shot, turn)
+    weight_in[pl.ds(shot, 1), :] = weight_out[pl.ds(own_cell, 1), :]
+
     grad_first = to_variables(exchange_grad(grad_update, saved_one))
-    grad_prior = [a + b + c for a, b, c in zip(cot, grad_total, grad_first)]
-
     for half in range(2):
+        grad_prior = cot[half] + grad_total[half] + grad_first[half]
         for t in range(16):
-            part_out[pl.ds(t * 16 + half, 1), :] = marginal[half][t]
-            part_out[pl.ds(t * 16 + 2 + half, 1), :] = grad_prior[half][t]
-    for t in range(16):
-        part_out[pl.ds(t * 16 + 8, 8), :] = grad_weight[t * 8 : t * 8 + 8, :]
-    own = pl.ds(pl.multiple_of(j * 16, 16), 16)
-    part_in[own, :] = part_out[own, :]
-    send("var", 3, lambda t: part_out.at[pl.ds(pl.multiple_of(t * 16, 16), 16)], part_in, 16)
-    await_all(recv_sem, 3, part_in, 16, 16)
+            late_out[pl.ds(t, 1), pl.ds(half * 128, 128)] = grad_prior[t]
+    for turn in everyone:
+        other = lax.bitwise_xor(j, turn % 16)
+        send(6, late_out.at[pl.ds(other, 1)], late_in, shot, turn)
+    late_in[pl.ds(shot, 1), :] = late_out[pl.ds(j, 1), :]
+
+    wait_for(recv_sem, 4, marg_in, 127)
     for half in range(2):
-        sum_out[pl.ds(half * 16, 16), :] = part_in[pl.ds(half, 16, stride=16), :]
-    weight_sum = part_in[8:16, :]
-    for t in range(1, 16):
-        weight_sum = weight_sum + part_in[pl.ds(t * 16 + 8, 8), :]
-    sum_out[pl.ds(32, 8), :] = weight_sum
-    for half in range(2):
-        sum_out[pl.ds(40 + half, 1), :] = jnp.sum(
-            part_in[pl.ds(2 + half, 16, stride=16), :], axis=0, keepdims=True
+        marg_ref[pl.ds(half * 128, 128), :] = jnp.transpose(
+            marg_in[:, half * 128 : half * 128 + 128]
         )
-    own = pl.ds(pl.multiple_of(i * 48, 16), 48)
-    sum_in[own, :] = sum_out[...]
-    send("chk", 4, lambda t: sum_out, sum_in, 48)
-    await_all(recv_sem, 4, sum_in, 48, 8)
-    await_all(send_sem, 0, cell_out, 8, 16)
-    await_all(send_sem, 1, sigma_in, 16, 8)
-    await_all(send_sem, 2, block_in, 64, 8)
-    await_all(send_sem, 3, part_out, 16, 16)
-    await_all(send_sem, 4, sum_in, 48, 8)
-
-
-def finish_kernel(sum_in, row_hot_ref, lane_hot_ref, marg_ref, wgrad_ref, pgrad_ref):
-    i = lax.axis_index("chk")
-    for half in range(2):
-        rows = jnp.concatenate(
-            [sum_in[pl.ds(t * 48 + half * 16, 16), :] for t in range(8)], axis=0
-        )
-        marg_ref[pl.ds(half * 128, 128), :] = jnp.transpose(rows)
-        pgrad_ref[pl.ds(half * 128, 128)] = jnp.sum(
-            sum_in[pl.ds(40 + half, 8, stride=48), :], axis=0
-        )
-    edge_grad = jnp.sum(sum_in[pl.ds(32 + i, 8, stride=48), :], axis=0, keepdims=True)
+    wait_for(recv_sem, 5, weight_in, 127)
+    edge_grad = jnp.sum(weight_in[...], axis=0, keepdims=True)
     spread = row_hot_ref[...] * edge_grad
     hot = lane_hot_ref[0:64, :]
     nothing = jnp.zeros((64, 128), F32)
@@ -639,39 +665,72 @@
     ) + exact_dot(spread[64:128, :], jnp.concatenate([nothing, hot], axis=0), ((1,), (1,)))
     for m in range(32):
         wgrad_ref[0, 0, :, pl.ds(m * 128, 128)] = dense[m * 2 : m * 2 + 2, :]
+    wait_for(recv_sem, 6, late_in, 127)
+    for half in range(2):
+        lanes = pl.ds(half * 128, 128)
+        pgrad_ref[lanes] = jnp.sum(late_in[:, half * 128 : half * 128 + 128], axis=0)
+
+    wait_for(send_sem, 0, cell_in, 127)
+    wait_for(send_sem, 1, prior_in, 15)
+    wait_for(send_sem, 2, sigma_in, 7)
+    wait_for(send_sem, 3, cot_in, 15)
+    wait_for(send_sem, 4, marg_in, 127)
+    wait_for(send_sem, 5, weight_in, 127)
+    wait_for(send_sem, 6, late_in, 127)
+
+
+def finish_kernel(marg_in, wgrad_in, pgrad_in, marg_out, wgrad_out, pgrad_out, sems):
+    copies = [
+        pltpu.make_async_copy(given, out, sems.at[at])
+        for at, (given, out) in enumerate(
+            ((marg_in, marg_out), (wgrad_in, wgrad_out), (pgrad_in, pgrad_out))
+        )
+    ]
+    for copy in copies:
+        copy.start()
+    for copy in copies:
+        copy.wait()
 
 
 VMEM_SPEC = pl.BlockSpec(memory_space=pltpu.VMEM)
 SMEM_SPEC = pl.BlockSpec(memory_space=pltpu.SMEM)
+ANY_SPEC = pl.BlockSpec(memory_space=pl.ANY)
 
 
 def sparse_parts(tile_bits, tile_pos, tile_count, edge_weight, syndrome, channel_prior, out_cot):
     shape = jax.ShapeDtypeStruct
+    held = [
+        pltpu.SMEM(tile_count.shape, jnp.int32),
+        pltpu.SMEM(tile_pos.shape, jnp.int32),
+        pltpu.VMEM(tile_bits.shape, jnp.int32),
+        pltpu.VMEM(edge_weight.shape, F32),
+        pltpu.VMEM(syndrome.shape, jnp.int32),
+        pltpu.VMEM(channel_prior.shape, F32),
+        pltpu.VMEM(out_cot.shape, F32),
+        pltpu.SemaphoreType.DMA((7,)),
+    ]
+    work = [(64, 128), (64, 128), (128, 128), (128, 128), (256, 128)]
+    exchanged = [
+        (1, 512), (128, 512), (1, 256), (16, 256), (8, 256), (8, 256), (16, 256), (16, 256),
+        (16, 256), (128, 256), (128, 128), (128, 128), (16, 256), (128, 256),
+    ]
     return pl.pallas_call(
         sparse_kernel,
         out_shape=(
-            shape((384, 128), F32),
-            shape((128, 128), F32),
-            shape((128, 128), F32),
+            shape(out_cot.shape, F32),
+            shape(edge_weight.shape, F32),
+            shape(channel_prior.shape, F32),
             shape((1, 1), F32),
         ),
-        in_specs=[SMEM_SPEC] * 2 + [VMEM_SPEC] * 5,
-        out_specs=(VMEM_SPEC, VMEM_SPEC, VMEM_SPEC, SMEM_SPEC),
-        scratch_shapes=[
-            pltpu.VMEM((64, 128), F32),
-            pltpu.VMEM((64, 128), F32),
-            pltpu.VMEM((256, 128), F32),
-            pltpu.VMEM((16, 128), F32),
-            pltpu.VMEM((128, 128), F32),
-            pltpu.VMEM((128, 128), F32),
-            pltpu.VMEM((128, 128), F32),
-            pltpu.VMEM((64, 128), F32),
-            pltpu.VMEM((512, 128), F32),
-            pltpu.VMEM((256, 128), F32),
-            pltpu.VMEM((256, 128), F32),
-            pltpu.VMEM((48, 128), F32),
-            pltpu.SemaphoreType.DMA((5,)),
-            pltpu.SemaphoreType.DMA((5,)),
+        in_specs=[ANY_SPEC] * 7,
+        out_specs=(VMEM_SPEC,) * 3 + (SMEM_SPEC,),
+        scratch_shapes=held
+        + [pltpu.VMEM(extent, F32) for extent in work + exchanged]
+        + [pltpu.VMEM((127, tiles, 128), F32) for tiles in (1, 2, 4)]
+        + [
+            pltpu.SemaphoreType.REGULAR,
+            pltpu.SemaphoreType.DMA((7,)),
+            pltpu.SemaphoreType.DMA((7,)),
         ],
         compiler_params=pltpu.CompilerParams(
             collective_id=0, has_side_effects=True, vmem_limit_bytes=48 << 20
@@ -679,18 +738,14 @@
     )(tile_count, tile_pos, tile_bits, edge_weight, syndrome, channel_prior, out_cot)
 
 
-def finish(parts, row_hot, lane_hot):
-    shape = jax.ShapeDtypeStruct
+def finish(*parts):
     return pl.pallas_call(
         finish_kernel,
-        out_shape=(
-            shape((256, 128), F32),
-            shape((1, 1, 2, 4096), F32),
-            shape((256,), F32),
-        ),
-        in_specs=[VMEM_SPEC] * 3,
-        out_specs=(VMEM_SPEC,) * 3,
-    )(parts, row_hot, lane_hot)
+        out_shape=tuple(jax.ShapeDtypeStruct(part.shape, part.dtype) for part in parts),
+        in_specs=[ANY_SPEC] * 3,
+        out_specs=(ANY_SPEC,) * 3,
+        scratch_shapes=[pltpu.SemaphoreType.DMA((3,))],
+    )(*parts)
 
 
 def body(*arguments):

time: 40.6 us -> 35 us (0.86)
  Pallas kernels: 37.9 us -> 32.1 us
    pallas_call x2, Pallas kernels: 37.9 us -> 32.1 us  [the longest x1 31.4 us: sparse_parts(): pl.pallas_call(sparse_kernel, out_shape=(shape(out_cot.shape, F32), shape...]
where the time goes in v3:
time: 35 us; the launch traced here: 34.9 us
  Pallas kernels  32.1 us (92%)
  between operations  1.98 us (6%)
  local copies, waits for them, and re-layouts  0.56 us (2%)
    pallas_call x1, Pallas kernels, sparse_parts(): pl.pallas_call(sparse_kernel, out_shape=(shape(out_cot.shape, F32), shape...  31.4 us

profile of v3, /device:TPU:1, one launch (start us, length us, event | category | flops | bytes accessed | tf_op | source)
XLA Modules:
  0.0 34.9 jit_solution(7718988891143729431)
XLA Ops:
  1.3 31.4 %shard_map.100 = (f32[256,128]{1,0:T(8,128)S(1)}, f32[1,1,2,4096]{3,2,1,0:T(2,128)S(1)}, f32[256]{0:T(256)S(1)}, f32[1,1]{1,0:T(1,128)}) custom-call(s32[1,1]{1,0:T(1,128)S(6)} %copy.404.count_hbm, s32[1,1,2,2]{3,2,1,0:T(2,128)} %pos_hbm.1, s32[1,1,2,4096]{3,2,1,0:T(2,128)} %bits_hbm.1, f32[1,1,2,4096]{3,2,1,0:T(2,128)} %weight_hbm.1, ...), custom_call_target="tpu_custom_call" | custom-call | tf_op jit(solution)/shard_map/pallas_call | solution.py:717
  33.4 0.9 %conditional.1 = ((f32[256,128]{1,0:T(8,128)}, f32[1,1,2,4096]{3,2,1,0:T(2,128)}, f32[256]{0:T(256)S(1)})) conditional(s32[]{:T(128)} %bitcast.111, (f32[256,128]{1,0:T(8,128)S(1)}, f32[1,1,2,4096]{3,2,1,0:T(2,128)S(1)}, f32[256]{0:T(256)S(1)}) %tuple.23, (f32[256]{0:T(256)}, s32[1,1,2,2]{3,2,1,0:T(2,128)}, s32[1,1]{1,0:T(1,128)}, ...), branch_computations={%region_0.0_spmd, %region_1.46_spmd} | conditional | flops 258632576 | bytes 1007619712 | solution.py:753
  33.4 0.7 %branch_0_fun.1 = (f32[256,128]{1,0:T(8,128)}, f32[1,1,2,4096]{3,2,1,0:T(2,128)}, f32[256]{0:T(256)S(1)}) custom-call(f32[256,128]{1,0:T(8,128)S(1)} %get-tuple-element.20.marg_in, f32[1,1,2,4096]{3,2,1,0:T(2,128)S(1)} %get-tuple-element.21.wgrad_in, f32[256]{0:T(256)S(1)} %get-tuple-element.22.pgrad_in), custom_call_target="tpu_custom_call" | custom-call | tf_op jit(solution)/shard_map/cond/branch_0_fun/pallas_call | solution.py:742
  34.3 0.0 copy-start.133
  34.3 0.6 %copy-done.133 = f32[256]{0:T(256)} copy-done((f32[256]{0:T(256)}, f32[256]{0:T(256)S(1)}, u32[]{:S(2)}) %copy-start.133) | copy-done | bytes 1048
Async XLA Ops:
  34.3 0.6 %copy-start.133 = (f32[256]{0:T(256)}, f32[256]{0:T(256)S(1)}, u32[]{:S(2)}) copy-start(f32[256]{0:T(256)S(1)} %get-tuple-element.458) | copy-start | bytes 3076

commit v4 on v3

--- a/solution.py
+++ b/solution.py
@@ -287,16 +287,23 @@
 
 def last_places(order):
     out = []
+    marks = [
+        jnp.broadcast_to(order[:, at : at + 1], (128, 128)) for at in range(15, 128, 16)
+    ]
     for half in range(2):
         key = (iota((128, 128), 1) + 128 * half).astype(F32)
         place = jnp.zeros((128, 128), jnp.int32)
         seen = jnp.full((128, 128), -1.0, F32)
-        for step in (64, 32, 16, 8, 4, 2, 1, 1):
-            value = take(order, place + (step - 1))
+        for mark in marks:
+            fits = mark <= key
+            place = jnp.where(fits, place + 16, place)
+            seen = jnp.where(fits, mark, seen)
+        for step in (8, 4, 2, 1):
+            value = take(order, jnp.minimum(place + (step - 1), 127))
             fits = value <= key
             place = jnp.where(fits, place + step, place)
             seen = jnp.where(fits, value, seen)
-        out.append((jnp.maximum(place - 1, 0), seen == key))
+        out.append((jnp.clip(place - 1, 0, 127), seen == key))
     return out
 
 
@@ -358,20 +365,12 @@
     raw_bits, raw_weight, row_hot_ref, lane_hot_ref, flip_ref,
     cell_out, cell_in, prior_out, prior_in, sigma_out, sigma_in, cot_out, cot_in,
     marg_out, marg_in, weight_out, weight_in, late_out, late_in,
-    size_1, size_2, size_4, entered, send_sem, recv_sem,
+    size_1, size_2, size_4, send_sem, recv_sem,
 ):
     row_sizes = {1: size_1, 2: size_2, 4: size_4}
     i = lax.axis_index("chk")
     j = lax.axis_index("var")
     barrier = pltpu.get_barrier_semaphore()
-    for step in range(1, 16):
-        pl.semaphore_signal(
-            barrier, 1, device_id={"var": lax.rem(j + step, 16)}, device_id_type=MESH_ID
-        )
-    for step in range(1, 8):
-        pl.semaphore_signal(
-            barrier, 1, device_id={"chk": lax.rem(i + step, 8)}, device_id_type=MESH_ID
-        )
     loads = [
         pltpu.make_async_copy(given, held, load_sem.at[at])
         for at, (given, held) in enumerate(
@@ -388,6 +387,18 @@
     ]
     for load in loads:
         load.start()
+    everyone = sorted(range(1, 128), key=lambda turn: -bin(turn).count("1"))
+    of_row = [turn for turn in everyone if turn < 16]
+    of_column = [turn for turn in everyone if turn % 16 == 0]
+
+    def device(turn):
+        return {
+            "chk": lax.bitwise_xor(i, turn // 16),
+            "var": lax.bitwise_xor(j, turn % 16),
+        }
+
+    for turn in everyone:
+        pl.semaphore_signal(barrier, 1, device_id=device(turn), device_id_type=MESH_ID)
 
     def send(phase, source, target, row, turn):
         pltpu.make_async_remote_copy(
@@ -395,16 +406,9 @@
             dst_ref=target.at[pl.ds(row, 1)],
             send_sem=send_sem.at[phase],
             recv_sem=recv_sem.at[phase],
-            device_id={
-                "chk": lax.bitwise_xor(i, turn // 16),
-                "var": lax.bitwise_xor(j, turn % 16),
-            },
+            device_id=device(turn),
             device_id_type=MESH_ID,
         ).start()
-
-    everyone = sorted(range(1, 128), key=lambda turn: -bin(turn).count("1"))
-    of_row = [turn for turn in everyone if turn < 16]
-    of_column = [turn for turn in everyone if turn % 16 == 0]
 
     def wait_for(sems, phase, target, count):
         whole = row_sizes[target.shape[1] // 128].at[pl.ds(0, count)]
@@ -466,15 +470,6 @@
     weight_at = exact_dot(weights, row_hot, ((0,), (0,)))
     edge_weight = jnp.sum(weight_at * lane_hot, axis=0, keepdims=True)
 
-    pl.semaphore_wait(barrier, 22)
-    for turn in of_column:
-        pl.semaphore_signal(
-            entered,
-            1,
-            device_id={"chk": lax.bitwise_xor(i, turn // 16)},
-            device_id_type=MESH_ID,
-        )
-
     def turned(values):
         flipped = jnp.transpose(values)[0:64, :]
         odd = (iota((64, 128), 1) & 1) == 1
@@ -489,7 +484,7 @@
     place_at = small_dot(marks_turned * turned(place), col_hot, ((0,), (0,)))
     order = jnp.sum(place_at * down_hot, axis=0, keepdims=True)
 
-    pl.semaphore_wait(entered, 7)
+    pl.semaphore_wait(barrier, 127)
 
     own_cell = j * 8 + i
     shot = i * 16 + j
@@ -728,7 +723,6 @@
         + [pltpu.VMEM(extent, F32) for extent in work + exchanged]
         + [pltpu.VMEM((127, tiles, 128), F32) for tiles in (1, 2, 4)]
         + [
-            pltpu.SemaphoreType.REGULAR,
             pltpu.SemaphoreType.DMA((7,)),
             pltpu.SemaphoreType.DMA((7,)),
         ],

time: 35 us -> 34.1 us (0.974)
  Pallas kernels: 32.1 us -> 31.2 us
    pallas_call x1, Pallas kernels: 31.4 us -> 30.5 us  [sparse_parts(): pl.pallas_call(sparse_kernel, out_shape=(shape(out_cot.shape, F32), shape...]
where the time goes in v4:
time: 34.1 us; the launch traced here: 33.9 us
  Pallas kernels  31.2 us (91%)
  between operations  1.98 us (6%)
  local copies, waits for them, and re-layouts  0.56 us (2%)
    pallas_call x1, Pallas kernels, sparse_parts(): pl.pallas_call(sparse_kernel, out_shape=(shape(out_cot.shape, F32), shape...  30.5 us
    pallas_call x1, Pallas kernels, finish(): pl.pallas_call(finish_kernel, out_shape=tuple((jax.ShapeDtypeStruct(part....  0.69 us

profile of v4, /device:TPU:1, one launch (start us, length us, event | category | flops | bytes accessed | tf_op | source)
XLA Modules:
  0.0 33.9 jit_solution(2916581430507941372)
XLA Ops:
  1.3 30.5 %shard_map.100 = (f32[256,128]{1,0:T(8,128)S(1)}, f32[1,1,2,4096]{3,2,1,0:T(2,128)S(1)}, f32[256]{0:T(256)S(1)}, f32[1,1]{1,0:T(1,128)}) custom-call(s32[1,1]{1,0:T(1,128)S(6)} %copy.404.count_hbm, s32[1,1,2,2]{3,2,1,0:T(2,128)} %pos_hbm.1, s32[1,1,2,4096]{3,2,1,0:T(2,128)} %bits_hbm.1, f32[1,1,2,4096]{3,2,1,0:T(2,128)} %weight_hbm.1, ...), custom_call_target="tpu_custom_call" | custom-call | tf_op jit(solution)/shard_map/pallas_call | solution.py:712
  32.4 0.9 %conditional.1 = ((f32[256,128]{1,0:T(8,128)}, f32[1,1,2,4096]{3,2,1,0:T(2,128)}, f32[256]{0:T(256)S(1)})) conditional(s32[]{:T(128)} %bitcast.111, (f32[256,128]{1,0:T(8,128)S(1)}, f32[1,1,2,4096]{3,2,1,0:T(2,128)S(1)}, f32[256]{0:T(256)S(1)}) %tuple.23, (f32[256]{0:T(256)}, s32[1,1,2,2]{3,2,1,0:T(2,128)}, s32[1,1]{1,0:T(1,128)}, ...), branch_computations={%region_0.0_spmd, %region_1.46_spmd} | conditional | flops 258632576 | bytes 1007619712 | solution.py:747
  32.5 0.7 %branch_0_fun.1 = (f32[256,128]{1,0:T(8,128)}, f32[1,1,2,4096]{3,2,1,0:T(2,128)}, f32[256]{0:T(256)S(1)}) custom-call(f32[256,128]{1,0:T(8,128)S(1)} %get-tuple-element.20.marg_in, f32[1,1,2,4096]{3,2,1,0:T(2,128)S(1)} %get-tuple-element.21.wgrad_in, f32[256]{0:T(256)S(1)} %get-tuple-element.22.pgrad_in), custom_call_target="tpu_custom_call" | custom-call | tf_op jit(solution)/shard_map/cond/branch_0_fun/pallas_call | solution.py:736
  33.4 0.0 copy-start.133
  33.4 0.6 %copy-done.133 = f32[256]{0:T(256)} copy-done((f32[256]{0:T(256)}, f32[256]{0:T(256)S(1)}, u32[]{:S(2)}) %copy-start.133) | copy-done | bytes 1048
Async XLA Ops:
  33.4 0.6 %copy-start.133 = (f32[256]{0:T(256)}, f32[256]{0:T(256)S(1)}, u32[]{:S(2)}) copy-start(f32[256]{0:T(256)S(1)} %get-tuple-element.458) | copy-start | bytes 3076
